TPU v7x, 128 devices: a whole 4x4x4 slice. The times are simulated.
128 devices in a mesh: zone: 16 (over x, z), tile: 8 (over y, core).
Axes of the slice: x: 4, y: 4, z: 4, core: 2. Of those that a mesh axis runs over, the one named last changes fastest.
Arguments:
- a_coord: float32 [2, 4194304], P(None, ('zone', 'tile')), may hold values from -6 to 6
- a_var: float32 [4194304], P(('zone', 'tile')), may hold values from 0.1 to 1
- dest: int32 [32768, 1], P(('zone', 'tile')), may hold values from 0 to 127; in each aligned block of 256 rows (0 to 255, 256 to 511, ...) at most 4 rows name the same one
- cand: int32 [32768, 4], P(('zone', 'tile')), may hold values from 0 to 79
- cand_count: int32 [32768, 1], P(('zone', 'tile')), may hold values from 1 to 4
- b_coord: float32 [2, 1048576], P(None, ('zone', 'tile')), may hold values from -6 to 6
- b_var: float32 [1048576], P(('zone', 'tile')), may hold values from 0.1 to 1
- b_prior: float32 [1048576], P(('zone', 'tile')), may hold values from 0.002 to 0.02
- b_flux: float32 [3, 1048576], P(None, ('zone', 'tile')), may hold values from -6 to 6
Outputs:
- matched: float32 [5, 4194304], P(None, ('zone', 'tile'))
- match_prob: float32 [4194304], P(('zone', 'tile'))
Inputs may be any that keep to these rules, and one draw needn't show every extreme that they name: `dest`: among the 256 blocks of one device, at most 4 name any one owner device, a bound that some block reaches.
All inputs are finite; a program needn't handle non-finite values.
Results may differ from a plain program's by a relative error of at most 0.0003.
Values sent between devices are 32-bit elements; how exact they have to be, the bound alone decides.
A program may use at most 64 MiB of HBM per device.

v0:
```python
from functools import partial

import jax
import jax.numpy as jnp
from jax import lax
from jax.sharding import PartitionSpec as P

TB = 128
K = 4
MB = 8


def padded(array, sides, width):
    for axis, dim in sides:
        size, length = (lax.axis_size(axis), array.shape[dim])
        up = [(i, (i + 1) % size) for i in range(size - 1)]
        down = [(j, i) for i, j in up]
        last = lax.slice_in_dim(array, length - width, length, axis=dim)
        first = lax.slice_in_dim(array, 0, width, axis=dim)
        before = lax.ppermute(last, axis, up)
        after = lax.ppermute(first, axis, down)
        array = jnp.concatenate([before, array, after], axis=dim)
    return array


def slot_match(a_block, candidates, live_count):
    numerator = jnp.zeros((5, a_block.shape[1]), jnp.float32)
    weight_sum = jnp.zeros((a_block.shape[1],), jnp.float32)
    for position in range(len(candidates)):
        block_data = candidates[position]
        is_live = jnp.where(live_count > position, 1.0, 0.0).astype(jnp.float32)
        delta_u = a_block[0][:, None] - block_data[0][None, :]
        delta_v = a_block[1][:, None] - block_data[1][None, :]
        var_sum = a_block[2][:, None] + block_data[5][None, :]
        weight = (
            (block_data[6] * is_live)[None, :]
            * (2.0 / var_sum)
            * jnp.exp(-(delta_u * delta_u + delta_v * delta_v) / (2.0 * var_sum))
        )
        numerator = numerator + jnp.einsum(
            "fj,ij->fi", block_data[:5], weight, precision=lax.Precision.HIGHEST
        )
        weight_sum = weight_sum + jnp.sum(weight, axis=1)
    inverse = 1.0 / (1.0 + weight_sum)
    return jnp.concatenate([numerator * inverse[None, :], (weight_sum * inverse)[None, :]], axis=0)


def match_one(window, items):
    a_block, labels = items
    candidates = []
    for position in range(K):
        block_index = labels[position].astype(jnp.int32)
        candidates.append(window[block_index])
    return slot_match(a_block, candidates, labels[K])


def match_many(window, pieces):
    floats, labels = pieces
    leading = floats.shape[:-2]
    results = lax.map(
        partial(match_one, window),
        (floats.reshape(-1, 3, TB), labels.reshape(-1, K + 1)),
        batch_size=128,
    )
    return results.reshape(leading + (6, TB))


def body(a_coord, a_var, dest, cand, cand_count, b_coord, b_var, b_prior, b_flux):
    zone_count = lax.axis_size("zone")
    tile_count = lax.axis_size("tile")
    devices = zone_count * tile_count
    blocks_here = dest.shape[0]
    capacity = max(2, (2 * blocks_here + devices - 1) // devices)
    b_stack = jnp.concatenate([b_coord, b_flux, b_var[None, :], b_prior[None, :]], axis=0)
    window = padded(b_stack, (("zone", 1),), MB * TB)
    window = window.reshape(7, -1, TB).transpose(1, 0, 2)
    a_stack = (
        jnp.concatenate([a_coord, a_var[None, :]], axis=0)
        .reshape(3, blocks_here, TB)
        .transpose(1, 0, 2)
    )
    labels = jnp.concatenate([cand, cand_count], axis=1).astype(jnp.float32)
    target = dest[:, 0]
    onehot = (target[:, None] == jnp.arange(devices, dtype=jnp.int32)[None, :]).astype(jnp.int32)
    slot_rank = jnp.sum(jnp.cumsum(onehot, axis=0) * onehot, axis=1) - 1
    slot_index = target * capacity + slot_rank
    send_floats = jnp.zeros((devices * capacity, 3, TB), jnp.float32).at[slot_index].set(a_stack)
    send_labels = jnp.zeros((devices * capacity, K + 1), jnp.float32).at[slot_index].set(labels)
    matcher = partial(match_many, window)
    results = matcher(
        (
            lax.all_to_all(
                send_floats.reshape(devices, capacity, 3, TB),
                ("zone", "tile"),
                split_axis=0,
                concat_axis=0,
                tiled=True,
            ),
            lax.all_to_all(
                send_labels.reshape(devices, capacity, K + 1),
                ("zone", "tile"),
                split_axis=0,
                concat_axis=0,
                tiled=True,
            ),
        )
    )
    returned = lax.all_to_all(
        results, ("zone", "tile"), split_axis=0, concat_axis=0, tiled=True
    ).reshape(devices * capacity, 6, TB)
    returned = returned[slot_index].transpose(1, 0, 2).reshape(6, blocks_here * TB)
    return (returned[:5], returned[5])


def solution(mesh):
    placed = (
        P(None, ("zone", "tile")),
        P(("zone", "tile")),
        P(("zone", "tile"), None),
        P(("zone", "tile"), None),
        P(("zone", "tile"), None),
        P(None, ("zone", "tile")),
        P(("zone", "tile")),
        P(("zone", "tile")),
        P(None, ("zone", "tile")),
    )
    return jax.shard_map(
        body,
        mesh=mesh,
        in_specs=placed,
        out_specs=(P(None, ("zone", "tile")), P(("zone", "tile"))),
        check_vma=False,
    )
```

profile of v0, /device:TPU:1, one launch (start us, length us, event | category | flops | bytes accessed | tf_op | source)
XLA Modules:
  0.0 599.1 jit_solution(10256650140271910987)
XLA Ops:
  0.6 0.8 copy.31
  1.7 0.9 fusion.66
  2.6 0.7 compare_select_fusion.8
  3.3 0.7 add_convert_fusion
  4.1 1.8 scatter_custom_fusion
  5.9 11.5 %all-to-all-start = ((f32[128,4,5]{2,1,0:T(4,128)}), f32[128,4,5]{2,1,0:T(4,128)S(1)}, u32[]{:S(2)}, u32[]{:S(2)}) async-start(f32[128,4,5]{2,1,0:T(4,128)} %bitcast.38), calls=%async_computation | async-start | bytes 524288 | tf_op jit(solution)/shard_map/all_to_all | solution.py:99
  17.5 1.3 maximum_bitcast_fusion.1
  18.9 7.0 %scatter_fusion = f32[512,3,128]{2,1,0:T(4,128)S(1)} fusion(f32[512,3,128]{2,1,0:T(4,128)S(1)} %broadcast_in_dim.54, s32[256]{0:T(256)S(1)} %bitcast.182, f32[256,3,128]{2,1,0:T(4,128)S(1)} %maximum_bitcast_fusion.1), kind=kCustom, calls=%fused_computation.6 | custom fusion | bytes 1180672 | tf_op jit(solution)/shard_map/scatter | solution.py:87
  25.9 1.1 copy.36
  27.0 1.3 all-to-all-done
  28.2 8.5 %all-to-all-start.1 = ((f32[128,4,3,128]{3,1,2,0:T(4,128)}), f32[128,4,3,128]{3,1,2,0:T(4,128)S(1)}, u32[]{:S(2)}, u32[]{:S(2)}) async-start(f32[128,4,3,128]{3,1,2,0:T(4,128)} %copy.36), calls=%async_computation.1 | async-start | bytes 1572864 | tf_op jit(solution)/shard_map/all_to_all | solution.py:92
  36.8 3.4 collective-permute-start
  40.2 1.3 collective-permute-start.1
  41.7 3.8 collective-permute-done
  45.4 2.6 collective-permute-done.1
  48.2 4.9 all-to-all-done.1
  53.3 507.4 %while.10 = (s32[]{:T(128)}, f32[4,128,6,128]{3,2,1,0:T(8,128)}, f32[4,128,5]{1,2,0:T(8,128)S(1)}, f32[80,7,128]{2,1,0:T(8,128)S(1)}, f32[4,128,3,128]{3,1,0,2:T(8,128)S(1)}, /*index=5*/s32[]{:T(128)}) while((s32[]{:T(128)}, f32[4,128,6,128]{3,2,1,0:T(8,128)}, f32[4,128,5]{1,2,0:T(8,128)S(1)}, f32[80,7,128]{2,1,0:T(8,128)S(1)}, ...), condition=%wide.region_10.11_spmd, body=%wide.region_5.0_spmd.sunk | while | flops 713592832 | bytes 16863336 | solution.py:60
  53.3 0.8 gather_fusion.1
  54.1 0.8 gather_fusion
  55.6 21.2 %fusion.99 = f32[128,5,128]{2,1,0:T(8,128)} fusion(f32[128,128]{1,0:T(8,128)S(1)} %bitcast.142, f32[128,128]{1,0:T(8,128)S(1)} %bitcast.138, f32[128,128]{1,0:T(8,128)S(1)} %bitcast.140, f32[128,128]{1,0:T(8,128)S(1)} %bitcast.136, f32[128,128]{1,0:T(8,128)S(1)} %get-tuple-element.167, f32[128,128]{1,0:T(8,128)S(1)} %get-tuple-element.169, ...), kind=kOutput, calls=%fused_computation.36.clone.1 | convolution fusion | flops 150994944 | bytes 1245184 | tf_op jit(solution)/shard_map/while/body/eval_jaxpr/vmap(fj,ij->fi)/dot_general | solution.py:40
  76.8 0.8 gather_fusion.2
  77.7 0.8 gather_fusion.3
  79.1 23.8 %fusion.98 = f32[128,5,128]{2,1,0:T(8,128)S(1)} fusion(f32[128,128]{1,0:T(8,128)S(1)} %bitcast.160, f32[128,128]{1,0:T(8,128)S(1)} %bitcast.164, f32[128,128]{1,0:T(8,128)S(1)} %bitcast.162, f32[128,128]{1,0:T(8,128)S(1)} %bitcast.166, f32[128,128]{1,0:T(8,128)S(1)} %get-tuple-element.167, f32[128,128]{1,0:T(8,128)S(1)} %get-tuple-element.169, ...), kind=kOutput, calls=%fused_computation.34.clone.1 | convolution fusion | flops 150994944 | bytes 1245184 | tf_op jit(solution)/shard_map/while/body/eval_jaxpr/vmap(fj,ij->fi)/dot_general | solution.py:40
  102.9 23.9 %fusion.100 = f32[128,5,128]{2,1,0:T(8,128)S(1)} fusion(f32[128,5,128]{2,1,0:T(8,128)S(1)} %fusion.98, f32[128,5,128]{2,1,0:T(8,128)S(1)} %copy-done.6, f32[128,128]{1,0:T(8,128)S(1)} %bitcast.144, f32[128,128]{1,0:T(8,128)S(1)} %get-tuple-element.167, f32[128,128]{1,0:T(8,128)S(1)} %bitcast.148, f32[128,128]{1,0:T(8,128)S(1)} %get-tuple-element.169, ...), kind=kOutput, calls=%fused_computation.40.clone.1 | convolution fusion | flops 151158784 | bytes 1900544 | tf_op jit(solution)/shard_map/while/body/eval_jaxpr/vmap(fj,ij->fi)/dot_general | solution.py:40
  126.8 28.3 %fusion.97 = (f32[128,128]{1,0:T(8,128)S(1)}, f32[128,128]{1,0:T(8,128)S(1)}, f32[128,128]{1,0:T(8,128)S(1)}, f32[128,128]{1,0:T(8,128)S(1)}) fusion(f32[128,128]{1,0:T(8,128)S(1)} %bitcast.143, f32[128,128]{1,0:T(8,128)S(1)} %get-tuple-element.167, f32[128,128]{1,0:T(8,128)S(1)} %bitcast.139, f32[128,128]{1,0:T(8,128)S(1)} %get-tuple-element.169, ...), kind=kLoop, calls=%fused_computation.35.clone.1 | loop fusion | flops 108986368 | bytes 1507328 | tf_op jit(solution)/shard_map/while/body/eval_jaxpr/vmap()/reduce_sum | solution.py:43
  155.2 23.9 %fusion.101 = f32[128,5,128]{2,1,0:T(8,128)S(1)} fusion(f32[128,5,128]{2,1,0:T(8,128)S(1)} %fusion.100, f32[128,128]{1,0:T(8,128)S(1)} %bitcast.159, f32[128,128]{1,0:T(8,128)S(1)} %bitcast.155, f32[128,128]{1,0:T(8,128)S(1)} %bitcast.157, f32[128,128]{1,0:T(8,128)S(1)} %bitcast.153, f32[128,128]{1,0:T(8,128)S(1)} %get-tuple-element.167, ...), kind=kOutput, calls=%fused_computation.42.clone.1 | convolution fusion | flops 151158784 | bytes 1638400 | tf_op jit(solution)/shard_map/while/body/eval_jaxpr/vmap(fj,ij->fi)/dot_general | solution.py:40
  179.2 0.9 fusion.102
  180.1 0.8 gather_fusion.1
  181.0 0.8 gather_fusion
  182.4 21.2 %fusion.99 = f32[128,5,128]{2,1,0:T(8,128)} fusion(f32[128,128]{1,0:T(8,128)S(1)} %bitcast.142, f32[128,128]{1,0:T(8,128)S(1)} %bitcast.138, f32[128,128]{1,0:T(8,128)S(1)} %bitcast.140, f32[128,128]{1,0:T(8,128)S(1)} %bitcast.136, f32[128,128]{1,0:T(8,128)S(1)} %get-tuple-element.167, f32[128,128]{1,0:T(8,128)S(1)} %get-tuple-element.169, ...), kind=kOutput, calls=%fused_computation.36.clone.1 | convolution fusion | flops 150994944 | bytes 1245184 | tf_op jit(solution)/shard_map/while/body/eval_jaxpr/vmap(fj,ij->fi)/dot_general | solution.py:40
  203.7 0.8 gather_fusion.2
  204.5 0.8 gather_fusion.3
  205.9 23.8 %fusion.98 = f32[128,5,128]{2,1,0:T(8,128)S(1)} fusion(f32[128,128]{1,0:T(8,128)S(1)} %bitcast.160, f32[128,128]{1,0:T(8,128)S(1)} %bitcast.164, f32[128,128]{1,0:T(8,128)S(1)} %bitcast.162, f32[128,128]{1,0:T(8,128)S(1)} %bitcast.166, f32[128,128]{1,0:T(8,128)S(1)} %get-tuple-element.167, f32[128,128]{1,0:T(8,128)S(1)} %get-tuple-element.169, ...), kind=kOutput, calls=%fused_computation.34.clone.1 | convolution fusion | flops 150994944 | bytes 1245184 | tf_op jit(solution)/shard_map/while/body/eval_jaxpr/vmap(fj,ij->fi)/dot_general | solution.py:40
  229.7 23.9 %fusion.100 = f32[128,5,128]{2,1,0:T(8,128)S(1)} fusion(f32[128,5,128]{2,1,0:T(8,128)S(1)} %fusion.98, f32[128,5,128]{2,1,0:T(8,128)S(1)} %copy-done.6, f32[128,128]{1,0:T(8,128)S(1)} %bitcast.144, f32[128,128]{1,0:T(8,128)S(1)} %get-tuple-element.167, f32[128,128]{1,0:T(8,128)S(1)} %bitcast.148, f32[128,128]{1,0:T(8,128)S(1)} %get-tuple-element.169, ...), kind=kOutput, calls=%fused_computation.40.clone.1 | convolution fusion | flops 151158784 | bytes 1900544 | tf_op jit(solution)/shard_map/while/body/eval_jaxpr/vmap(fj,ij->fi)/dot_general | solution.py:40
  253.6 28.3 %fusion.97 = (f32[128,128]{1,0:T(8,128)S(1)}, f32[128,128]{1,0:T(8,128)S(1)}, f32[128,128]{1,0:T(8,128)S(1)}, f32[128,128]{1,0:T(8,128)S(1)}) fusion(f32[128,128]{1,0:T(8,128)S(1)} %bitcast.143, f32[128,128]{1,0:T(8,128)S(1)} %get-tuple-element.167, f32[128,128]{1,0:T(8,128)S(1)} %bitcast.139, f32[128,128]{1,0:T(8,128)S(1)} %get-tuple-element.169, ...), kind=kLoop, calls=%fused_computation.35.clone.1 | loop fusion | flops 108986368 | bytes 1507328 | tf_op jit(solution)/shard_map/while/body/eval_jaxpr/vmap()/reduce_sum | solution.py:43
  282.0 23.9 %fusion.101 = f32[128,5,128]{2,1,0:T(8,128)S(1)} fusion(f32[128,5,128]{2,1,0:T(8,128)S(1)} %fusion.100, f32[128,128]{1,0:T(8,128)S(1)} %bitcast.159, f32[128,128]{1,0:T(8,128)S(1)} %bitcast.155, f32[128,128]{1,0:T(8,128)S(1)} %bitcast.157, f32[128,128]{1,0:T(8,128)S(1)} %bitcast.153, f32[128,128]{1,0:T(8,128)S(1)} %get-tuple-element.167, ...), kind=kOutput, calls=%fused_computation.42.clone.1 | convolution fusion | flops 151158784 | bytes 1638400 | tf_op jit(solution)/shard_map/while/body/eval_jaxpr/vmap(fj,ij->fi)/dot_general | solution.py:40
  306.0 0.9 fusion.102
  307.0 0.8 gather_fusion.1
  307.8 0.8 gather_fusion
  309.3 21.2 %fusion.99 = f32[128,5,128]{2,1,0:T(8,128)} fusion(f32[128,128]{1,0:T(8,128)S(1)} %bitcast.142, f32[128,128]{1,0:T(8,128)S(1)} %bitcast.138, f32[128,128]{1,0:T(8,128)S(1)} %bitcast.140, f32[128,128]{1,0:T(8,128)S(1)} %bitcast.136, f32[128,128]{1,0:T(8,128)S(1)} %get-tuple-element.167, f32[128,128]{1,0:T(8,128)S(1)} %get-tuple-element.169, ...), kind=kOutput, calls=%fused_computation.36.clone.1 | convolution fusion | flops 150994944 | bytes 1245184 | tf_op jit(solution)/shard_map/while/body/eval_jaxpr/vmap(fj,ij->fi)/dot_general | solution.py:40
  330.5 0.8 gather_fusion.2
  331.3 0.8 gather_fusion.3
  332.8 23.8 %fusion.98 = f32[128,5,128]{2,1,0:T(8,128)S(1)} fusion(f32[128,128]{1,0:T(8,128)S(1)} %bitcast.160, f32[128,128]{1,0:T(8,128)S(1)} %bitcast.164, f32[128,128]{1,0:T(8,128)S(1)} %bitcast.162, f32[128,128]{1,0:T(8,128)S(1)} %bitcast.166, f32[128,128]{1,0:T(8,128)S(1)} %get-tuple-element.167, f32[128,128]{1,0:T(8,128)S(1)} %get-tuple-element.169, ...), kind=kOutput, calls=%fused_computation.34.clone.1 | convolution fusion | flops 150994944 | bytes 1245184 | tf_op jit(solution)/shard_map/while/body/eval_jaxpr/vmap(fj,ij->fi)/dot_general | solution.py:40
  356.6 23.9 %fusion.100 = f32[128,5,128]{2,1,0:T(8,128)S(1)} fusion(f32[128,5,128]{2,1,0:T(8,128)S(1)} %fusion.98, f32[128,5,128]{2,1,0:T(8,128)S(1)} %copy-done.6, f32[128,128]{1,0:T(8,128)S(1)} %bitcast.144, f32[128,128]{1,0:T(8,128)S(1)} %get-tuple-element.167, f32[128,128]{1,0:T(8,128)S(1)} %bitcast.148, f32[128,128]{1,0:T(8,128)S(1)} %get-tuple-element.169, ...), kind=kOutput, calls=%fused_computation.40.clone.1 | convolution fusion | flops 151158784 | bytes 1900544 | tf_op jit(solution)/shard_map/while/body/eval_jaxpr/vmap(fj,ij->fi)/dot_general | solution.py:40
  380.5 28.3 %fusion.97 = (f32[128,128]{1,0:T(8,128)S(1)}, f32[128,128]{1,0:T(8,128)S(1)}, f32[128,128]{1,0:T(8,128)S(1)}, f32[128,128]{1,0:T(8,128)S(1)}) fusion(f32[128,128]{1,0:T(8,128)S(1)} %bitcast.143, f32[128,128]{1,0:T(8,128)S(1)} %get-tuple-element.167, f32[128,128]{1,0:T(8,128)S(1)} %bitcast.139, f32[128,128]{1,0:T(8,128)S(1)} %get-tuple-element.169, ...), kind=kLoop, calls=%fused_computation.35.clone.1 | loop fusion | flops 108986368 | bytes 1507328 | tf_op jit(solution)/shard_map/while/body/eval_jaxpr/vmap()/reduce_sum | solution.py:43
  408.9 23.9 %fusion.101 = f32[128,5,128]{2,1,0:T(8,128)S(1)} fusion(f32[128,5,128]{2,1,0:T(8,128)S(1)} %fusion.100, f32[128,128]{1,0:T(8,128)S(1)} %bitcast.159, f32[128,128]{1,0:T(8,128)S(1)} %bitcast.155, f32[128,128]{1,0:T(8,128)S(1)} %bitcast.157, f32[128,128]{1,0:T(8,128)S(1)} %bitcast.153, f32[128,128]{1,0:T(8,128)S(1)} %get-tuple-element.167, ...), kind=kOutput, calls=%fused_computation.42.clone.1 | convolution fusion | flops 151158784 | bytes 1638400 | tf_op jit(solution)/shard_map/while/body/eval_jaxpr/vmap(fj,ij->fi)/dot_general | solution.py:40
  432.9 0.9 fusion.102
  433.8 0.8 gather_fusion.1
  434.6 0.8 gather_fusion
  436.1 21.2 %fusion.99 = f32[128,5,128]{2,1,0:T(8,128)} fusion(f32[128,128]{1,0:T(8,128)S(1)} %bitcast.142, f32[128,128]{1,0:T(8,128)S(1)} %bitcast.138, f32[128,128]{1,0:T(8,128)S(1)} %bitcast.140, f32[128,128]{1,0:T(8,128)S(1)} %bitcast.136, f32[128,128]{1,0:T(8,128)S(1)} %get-tuple-element.167, f32[128,128]{1,0:T(8,128)S(1)} %get-tuple-element.169, ...), kind=kOutput, calls=%fused_computation.36.clone.1 | convolution fusion | flops 150994944 | bytes 1245184 | tf_op jit(solution)/shard_map/while/body/eval_jaxpr/vmap(fj,ij->fi)/dot_general | solution.py:40
  457.4 0.8 gather_fusion.2
  458.2 0.8 gather_fusion.3
  459.6 23.8 %fusion.98 = f32[128,5,128]{2,1,0:T(8,128)S(1)} fusion(f32[128,128]{1,0:T(8,128)S(1)} %bitcast.160, f32[128,128]{1,0:T(8,128)S(1)} %bitcast.164, f32[128,128]{1,0:T(8,128)S(1)} %bitcast.162, f32[128,128]{1,0:T(8,128)S(1)} %bitcast.166, f32[128,128]{1,0:T(8,128)S(1)} %get-tuple-element.167, f32[128,128]{1,0:T(8,128)S(1)} %get-tuple-element.169, ...), kind=kOutput, calls=%fused_computation.34.clone.1 | convolution fusion | flops 150994944 | bytes 1245184 | tf_op jit(solution)/shard_map/while/body/eval_jaxpr/vmap(fj,ij->fi)/dot_general | solution.py:40
  483.4 23.9 %fusion.100 = f32[128,5,128]{2,1,0:T(8,128)S(1)} fusion(f32[128,5,128]{2,1,0:T(8,128)S(1)} %fusion.98, f32[128,5,128]{2,1,0:T(8,128)S(1)} %copy-done.6, f32[128,128]{1,0:T(8,128)S(1)} %bitcast.144, f32[128,128]{1,0:T(8,128)S(1)} %get-tuple-element.167, f32[128,128]{1,0:T(8,128)S(1)} %bitcast.148, f32[128,128]{1,0:T(8,128)S(1)} %get-tuple-element.169, ...), kind=kOutput, calls=%fused_computation.40.clone.1 | convolution fusion | flops 151158784 | bytes 1900544 | tf_op jit(solution)/shard_map/while/body/eval_jaxpr/vmap(fj,ij->fi)/dot_general | solution.py:40
  507.3 28.3 %fusion.97 = (f32[128,128]{1,0:T(8,128)S(1)}, f32[128,128]{1,0:T(8,128)S(1)}, f32[128,128]{1,0:T(8,128)S(1)}, f32[128,128]{1,0:T(8,128)S(1)}) fusion(f32[128,128]{1,0:T(8,128)S(1)} %bitcast.143, f32[128,128]{1,0:T(8,128)S(1)} %get-tuple-element.167, f32[128,128]{1,0:T(8,128)S(1)} %bitcast.139, f32[128,128]{1,0:T(8,128)S(1)} %get-tuple-element.169, ...), kind=kLoop, calls=%fused_computation.35.clone.1 | loop fusion | flops 108986368 | bytes 1507328 | tf_op jit(solution)/shard_map/while/body/eval_jaxpr/vmap()/reduce_sum | solution.py:43
  535.7 23.9 %fusion.101 = f32[128,5,128]{2,1,0:T(8,128)S(1)} fusion(f32[128,5,128]{2,1,0:T(8,128)S(1)} %fusion.100, f32[128,128]{1,0:T(8,128)S(1)} %bitcast.159, f32[128,128]{1,0:T(8,128)S(1)} %bitcast.155, f32[128,128]{1,0:T(8,128)S(1)} %bitcast.157, f32[128,128]{1,0:T(8,128)S(1)} %bitcast.153, f32[128,128]{1,0:T(8,128)S(1)} %get-tuple-element.167, ...), kind=kOutput, calls=%fused_computation.42.clone.1 | convolution fusion | flops 151158784 | bytes 1638400 | tf_op jit(solution)/shard_map/while/body/eval_jaxpr/vmap(fj,ij->fi)/dot_general | solution.py:40
  559.7 0.9 fusion.102
  560.6 3.1 copy.41
  563.8 4.8 all-to-all-start.2
  568.6 24.7 %all-to-all-done.2 = f32[128,4,6,128]{3,1,2,0:T(4,128)S(1)} async-done(((f32[128,4,6,128]{3,1,2,0:T(4,128)}), f32[128,4,6,128]{3,1,2,0:T(4,128)S(1)}, u32[]{:S(2)}, u32[]{:S(2)}) %all-to-all-start.2) | async-done | bytes 1572896 | tf_op jit(solution)/shard_map/all_to_all | solution.py:108
  593.3 1.7 copy.42
  594.9 2.3 gather_fusion.4
  597.3 1.0 slice_bitcast_fusion.3
  598.3 0.8 slice.161
  (72 shorter events, 6.1 us)
Async XLA Ops:
  3.3 23.7 %copy-start.4 = (s32[256,1]{0,1:T(1,128)}, s32[256,1]{0,1:T(1,128)S(1)}, u32[]{:S(2)}) copy-start(s32[256,1]{0,1:T(1,128)S(1)} %compare_select_fusion.8) | copy-start | bytes 3076
  5.9 22.3 %all-to-all-start = ((f32[128,4,5]{2,1,0:T(4,128)}), f32[128,4,5]{2,1,0:T(4,128)S(1)}, u32[]{:S(2)}, u32[]{:S(2)}) async-start(f32[128,4,5]{2,1,0:T(4,128)} %bitcast.38), calls=%async_computation | async-start | bytes 524288 | tf_op jit(solution)/shard_map/all_to_all | solution.py:99
  18.9 17.9 %copy-start = (f32[3,8192]{1,0:T(4,128)S(1)}, f32[3,8192]{1,0:T(4,128)}, u32[]{:S(2)}) copy-start(f32[3,8192]{1,0:T(4,128)} %param.19) | copy-start | bytes 294916
  18.9 17.9 %copy-start.1 = (f32[2,8192]{1,0:T(2,128)S(1)}, f32[2,8192]{1,0:T(2,128)}, u32[]{:S(2)}) copy-start(f32[2,8192]{1,0:T(2,128)} %param.16) | copy-start | bytes 196612
  18.9 17.9 %copy-start.2 = (f32[8192]{0:T(1024)S(1)}, f32[8192]{0:T(1024)}, u32[]{:S(2)}) copy-start(f32[8192]{0:T(1024)} %param.18) | copy-start | bytes 98308
  18.9 17.9 %copy-start.3 = (f32[8192]{0:T(1024)S(1)}, f32[8192]{0:T(1024)}, u32[]{:S(2)}) copy-start(f32[8192]{0:T(1024)} %param.17) | copy-start | bytes 98308
  28.2 24.9 %all-to-all-start.1 = ((f32[128,4,3,128]{3,1,2,0:T(4,128)}), f32[128,4,3,128]{3,1,2,0:T(4,128)S(1)}, u32[]{:S(2)}, u32[]{:S(2)}) async-start(f32[128,4,3,128]{3,1,2,0:T(4,128)} %copy.36), calls=%async_computation.1 | async-start | bytes 1572864 | tf_op jit(solution)/shard_map/all_to_all | solution.py:92
  36.8 8.6 %collective-permute-start = (f32[7,1024]{1,0:T(8,128)S(1)}, f32[7,1024]{1,0:T(8,128)S(1)}, u32[]{:S(2)}, u32[]{:S(2)}) collective-permute-start(f32[7,1024]{1,0:T(8,128)S(1)} %get-tuple-element.96), channel_id=1, source_target_pairs={{0,8},{8,16},{16,24},{24,32},{32,40},{40,48},{48,56},{56,64},{64,7... | collective-permute-start | bytes 86024 | tf_op jit(solution)/shard_map/ppermute | solution.py:20
  40.2 7.8 %collective-permute-start.1 = (f32[7,1024]{1,0:T(8,128)S(1)}, f32[7,1024]{1,0:T(8,128)S(1)}, u32[]{:S(2)}, u32[]{:S(2)}) collective-permute-start(f32[7,1024]{1,0:T(8,128)S(1)} %get-tuple-element.97), channel_id=1, source_target_pairs={{8,0},{16,8},{24,16},{32,24},{40,32},{48,40},{56,48},{64,56},{72,6... | collective-permute-start | bytes 86024 | tf_op jit(solution)/shard_map/ppermute | solution.py:21
  79.1 23.8 %copy-start.6 = (f32[128,5,128]{2,1,0:T(8,128)S(1)}, f32[128,5,128]{2,1,0:T(8,128)}, u32[]{:S(2)}) copy-start(f32[128,5,128]{2,1,0:T(8,128)} %fusion.99) | copy-start | bytes 983044 | tf_op jit(solution)/shard_map/while
  205.9 23.8 %copy-start.6 = (f32[128,5,128]{2,1,0:T(8,128)S(1)}, f32[128,5,128]{2,1,0:T(8,128)}, u32[]{:S(2)}) copy-start(f32[128,5,128]{2,1,0:T(8,128)} %fusion.99) | copy-start | bytes 983044 | tf_op jit(solution)/shard_map/while
  332.7 23.8 %copy-start.6 = (f32[128,5,128]{2,1,0:T(8,128)S(1)}, f32[128,5,128]{2,1,0:T(8,128)}, u32[]{:S(2)}) copy-start(f32[128,5,128]{2,1,0:T(8,128)} %fusion.99) | copy-start | bytes 983044 | tf_op jit(solution)/shard_map/while
  459.6 23.8 %copy-start.6 = (f32[128,5,128]{2,1,0:T(8,128)S(1)}, f32[128,5,128]{2,1,0:T(8,128)}, u32[]{:S(2)}) copy-start(f32[128,5,128]{2,1,0:T(8,128)} %fusion.99) | copy-start | bytes 983044 | tf_op jit(solution)/shard_map/while
  563.8 4.8 copy-start.5
  563.8 29.5 %all-to-all-start.2 = ((f32[128,4,6,128]{3,1,2,0:T(4,128)}), f32[128,4,6,128]{3,1,2,0:T(4,128)S(1)}, u32[]{:S(2)}, u32[]{:S(2)}) async-start(f32[128,4,6,128]{3,1,2,0:T(4,128)} %copy.41), calls=%async_computation.2 | async-start | bytes 3145728 | tf_op jit(solution)/shard_map/all_to_all | solution.py:108
where the time goes:
time: 600 us; the launch traced here: 599 us
  matrix products  371 us (62%)
  other arithmetic  126 us (21%)
  waiting for transfers between devices  37.3 us (6%)
  local copies, waits for them, and re-layouts  33.6 us (6%)
  starting transfers between devices  29.5 us (5%)
    dot_general x16, matrix products, slot_match(): jnp.einsum('fj,ij->fi', block_data[:5], weight, precision=lax.Precision.H...  371 us
    reduce_sum x4, other arithmetic, slot_match(): weight_sum = weight_sum + jnp.sum(weight, axis=1)  113 us
    all_to_all x1, waiting for transfers between devices, body(): lax.all_to_all(results, ('zone', 'tile'), split_axis=0, concat_axis=0, ti...  24.7 us
    gather x16, local copies, waits for them, and re-layouts, match_one(): candidates.append(window[block_index])  13.2 us
  transfers between devices with their start and end apart: 5, of which 5 were waited for; matrix products, arithmetic and copies ran while one was open for 2% of the time, Pallas kernels for 0%

commit v1 on v0

v1 whole, which is shorter than its diff:
```python
import functools
import math

import jax
import jax.numpy as jnp
from jax import lax
from jax.experimental import pallas as pl
from jax.experimental.pallas import tpu as pltpu
from jax.sharding import PartitionSpec as P

TB = 128
K = 4
MB = 8
CAP = 4
UNROLL = 16
SCALE = math.sqrt(0.5 / math.log(2.0))
F32 = jnp.float32
BF16 = jnp.bfloat16


def pack_kernel(dest, a_coord, a_var, labels, send, place, taken):
    devices = taken.shape[0]
    send[...] = jnp.zeros_like(send)

    def clear(i, c):
        taken[i] = 0
        return c

    lax.fori_loop(0, devices, clear, 0, unroll=8)

    def one(b, c):
        d = dest[b]
        r = taken[d]
        taken[d] = r + 1
        place[b] = d * 4 + r
        row = d * 16 + r
        lanes = pl.ds(pl.multiple_of(b * TB, TB), TB)
        send[pl.ds(row, 1), :] = a_coord[0:1, lanes]
        send[pl.ds(row + 4, 1), :] = a_coord[1:2, lanes]
        send[pl.ds(row + 8, 1), :] = a_var[pl.ds(b, 1), :]
        send[pl.ds(row + 12, 1), :] = labels[pl.ds(b, 1), :]
        return c

    lax.fori_loop(0, dest.shape[0], one, 0, unroll=4)


def match_kernel(labels, a_rows, window, out, wide, acc, todo):
    slots = a_rows.shape[0] // 4
    messages = slots // CAP
    blocks = window.shape[1] // TB
    steps = 16
    row = lax.broadcasted_iota(jnp.int32, (8, TB), 0)
    acc[...] = jnp.zeros_like(acc)

    def prepare(step, n):
        for k in range(blocks // steps):
            w = step * (blocks // steps) + k
            tile = window[:, pl.ds(pl.multiple_of(w * TB, TB), TB)]
            for q, line, gain in ((0, 0, SCALE), (1, 1, SCALE), (2, 5, 1.0)):
                wide[w, q] = jnp.broadcast_to(tile[line : line + 1] * gain, (TB, TB)).T
        for k in range(messages // steps * CAP):
            slot = step * (messages // steps * CAP) + k
            for p in range(K):
                todo[n + p] = slot * TB + labels[slot * 5 + p]
            n = n + labels[slot * 5 + K]
        return n

    pairs = lax.fori_loop(0, steps, prepare, 0)
    for k in range(UNROLL):
        todo[pairs + k] = slots * TB

    def pair(code):
        slot = jnp.minimum(code // TB, slots - 1)
        w = code % TB
        base = slot // CAP * 16 + slot % CAP
        tile = window[:, pl.ds(pl.multiple_of(w * TB, TB), TB)]
        du = wide[w, 0] - a_rows[pl.ds(base, 1), :] * SCALE
        dv = wide[w, 1] - a_rows[pl.ds(base + 4, 1), :] * SCALE
        r = pltpu.reciprocal(wide[w, 2] + a_rows[pl.ds(base + 8, 1), :], approx=True)
        weight = r * jnp.exp2((du * du + dv * dv) * -r)
        q = jnp.where(row == 5, 2.0, 2.0 * tile) * tile[6:7]
        q_high = q.astype(BF16).astype(F32)
        q = jnp.concatenate([q_high, q - q_high], axis=0).astype(BF16)
        high = weight.astype(BF16)
        low = (weight - high.astype(F32)).astype(BF16)
        total = jnp.dot(
            jnp.concatenate([q, q], axis=1),
            jnp.concatenate([high, low], axis=0),
            preferred_element_type=F32,
        )
        return total[0:8] + total[8:16]

    def chunk(c, carry):
        done = []
        for k in range(UNROLL):
            code = todo[c * UNROLL + k]
            done.append((code // TB, pair(code)))
        for slot, total in done:
            acc[slot] = acc[slot] + total
        return carry

    lax.fori_loop(0, (pairs + UNROLL - 1) // UNROLL, chunk, 0)

    def finish(m, carry):
        parts = []
        for r in range(CAP):
            total = acc[m * CAP + r]
            parts.append((total / (1.0 + total[5:6]))[0:6])
        out[m] = jnp.concatenate(parts, axis=0)
        return carry

    lax.fori_loop(0, messages, finish, 0, unroll=2)


def unpack_kernel(place, back, matched, prob):
    def one(b, c):
        slot = place[b]
        base = slot // CAP * 24 + slot % CAP * 6
        lanes = pl.ds(pl.multiple_of(b * TB, TB), TB)
        for q in range(5):
            matched[q : q + 1, lanes] = back[pl.ds(base + q, 1), :]
        prob[pl.ds(b, 1), :] = back[pl.ds(base + 5, 1), :]
        return c

    lax.fori_loop(0, place.shape[0], one, 0, unroll=4)


VMEM = pl.BlockSpec(memory_space=pltpu.VMEM)
SMEM = pl.BlockSpec(memory_space=pltpu.SMEM)


def params(mib):
    return pltpu.CompilerParams(vmem_limit_bytes=mib * 2**20)


def body(a_coord, a_var, dest, cand, cand_count, b_coord, b_var, b_prior, b_flux):
    zones = lax.axis_size("zone")
    devices = zones * lax.axis_size("tile")
    count = dest.shape[0]
    labels = jnp.concatenate([cand, cand_count], axis=1).astype(F32)
    labels = jnp.pad(labels, ((0, 0), (0, TB - K - 1)))
    send, place = pl.pallas_call(
        pack_kernel,
        out_shape=(
            jax.ShapeDtypeStruct((devices * 16, TB), F32),
            jax.ShapeDtypeStruct((count,), jnp.int32),
        ),
        in_specs=[SMEM, VMEM, VMEM, VMEM],
        out_specs=(VMEM, SMEM),
        scratch_shapes=[pltpu.SMEM((devices,), jnp.int32)],
        compiler_params=params(16),
        name="pack",
    )(dest.reshape(count), a_coord, a_var.reshape(count, TB), labels)
    got = lax.all_to_all(
        send.reshape(devices, 16, TB), ("zone", "tile"), split_axis=0, concat_axis=0, tiled=True
    )
    own = jnp.concatenate(
        [b_coord, b_flux, b_var[None, :], b_prior[None, :], jnp.zeros_like(b_var)[None, :]], axis=0
    )
    width = MB * TB
    up = [(i, i + 1) for i in range(zones - 1)]
    below = lax.ppermute(own[:, -width:], "zone", up)
    above = lax.ppermute(own[:, :width], "zone", [(j, i) for i, j in up])
    window = jnp.concatenate([below, own, above], axis=1)
    got_labels = got[:, 12:16, : K + 1].astype(jnp.int32).reshape(-1)
    slots = devices * CAP
    result = pl.pallas_call(
        match_kernel,
        out_shape=jax.ShapeDtypeStruct((devices, CAP * 6, TB), F32),
        in_specs=[SMEM, VMEM, VMEM],
        out_specs=VMEM,
        scratch_shapes=[
            pltpu.VMEM((window.shape[1] // TB, 3, TB, TB), F32),
            pltpu.VMEM((slots + 1, 8, TB), F32),
            pltpu.SMEM((slots * K + UNROLL + K,), jnp.int32),
        ],
        compiler_params=params(40),
        name="match",
    )(got_labels, got.reshape(devices * 16, TB), window)
    back = lax.all_to_all(result, ("zone", "tile"), split_axis=0, concat_axis=0, tiled=True)
    matched, prob = pl.pallas_call(
        unpack_kernel,
        out_shape=(
            jax.ShapeDtypeStruct((5, count * TB), F32),
            jax.ShapeDtypeStruct((count, TB), F32),
        ),
        in_specs=[SMEM, VMEM],
        out_specs=(VMEM, VMEM),
        compiler_params=params(16),
        name="unpack",
    )(place, back.reshape(slots * 6, TB))
    return matched, prob.reshape(count * TB)


def solution(mesh):
    both = ("zone", "tile")
    rows, columns, flat = P(both, None), P(None, both), P(both)
    return jax.shard_map(
        body,
        mesh=mesh,
        in_specs=(columns, flat, rows, rows, rows, columns, flat, flat, columns),
        out_specs=(columns, flat),
        check_vma=False,
    )
```

time: 600 us -> 138 us (0.23)
  matrix products: 371 us -> 0 us
  other arithmetic: 126 us -> 0.81 us
  blocking collectives: 0 us -> 49.8 us
  Pallas kernels: 0 us -> 45.5 us
  local copies, waits for them, and re-layouts: 33.6 us -> 4.12 us
  waiting for transfers between devices: 37.3 us -> 19 us
  starting transfers between devices: 29.5 us -> 17.3 us
    dot_general x16 -> x0, matrix products: 371 us -> none  [slot_match(): jnp.einsum('fj,ij->fi', block_data[:5], weight, precision=lax.Precision.H...]
    reduce_sum x5 -> x0, other arithmetic: 114 us -> none  [the longest x4 113 us: slot_match(): weight_sum = weight_sum + jnp.sum(weight, axis=1)]
    all_to_all x0 -> x1, blocking collectives: none -> 49.8 us  [body(): lax.all_to_all(result, ('zone', 'tile'), split_axis=0, concat_axis=0, til...]
    pallas_call x0 -> x3, Pallas kernels: none -> 45.5 us  [the longest x1 38.4 us: body(): pl.pallas_call(match_kernel, out_shape=jax.ShapeDtypeStruct((devices, CAP...]
    gather x17 -> x0, local copies, waits for them, and re-layouts: 15.5 us -> none  [the longest x16 13.2 us: match_one(): candidates.append(window[block_index])]
    all_to_all x3 -> x1, starting transfers between devices: 24.8 us -> 11.7 us  [body(): lax.all_to_all(send.reshape(devices, 16, TB), ('zone', 'tile'), split_axi...]
    all_to_all x3 -> x1, waiting for transfers between devices: 30.9 us -> 19 us  [body(): lax.all_to_all(send.reshape(devices, 16, TB), ('zone', 'tile'), split_axi...]
    scatter x2 -> x0, local copies, waits for them, and re-layouts: 8.78 us -> none  [the longest x1 6.97 us: body(): jnp.zeros((devices * capacity, 3, TB), jnp.float32).at[slot_index]]
  transfers between devices with their start and end apart: 5 -> 3, of which waited for: 5 -> 1; matrix products, arithmetic and copies ran while one was open for 2% -> 1% of each run, Pallas kernels for 0% -> 2%
where the time goes in v1:
time: 138 us; the launch traced here: 137 us
  blocking collectives  49.8 us (36%)
  Pallas kernels  45.5 us (33%)
  waiting for transfers between devices  19 us (14%)
  starting transfers between devices  17.3 us (13%)
  local copies, waits for them, and re-layouts  4.12 us (3%)
    all_to_all x1, blocking collectives, body(): lax.all_to_all(result, ('zone', 'tile'), split_axis=0, concat_axis=0, til...  49.8 us
    pallas_call x1, Pallas kernels, body(): pl.pallas_call(match_kernel, out_shape=jax.ShapeDtypeStruct((devices, CAP...  38.4 us
    all_to_all x1, waiting for transfers between devices, body(): lax.all_to_all(send.reshape(devices, 16, TB), ('zone', 'tile'), split_axi...  19 us
    all_to_all x1, starting transfers between devices, body(): lax.all_to_all(send.reshape(devices, 16, TB), ('zone', 'tile'), split_axi...  11.7 us
    ppermute x1, starting transfers between devices, body(): below = lax.ppermute(own[:, -width:], 'zone', up)  4.37 us
    pallas_call x1, Pallas kernels, body(): pl.pallas_call(unpack_kernel, out_shape=(jax.ShapeDtypeStruct((5, count *...  3.87 us
    pallas_call x1, Pallas kernels, body(): pl.pallas_call(pack_kernel, out_shape=(jax.ShapeDtypeStruct((devices * 16...  3.23 us
  transfers between devices with their start and end apart: 3, of which 1 were waited for; matrix products, arithmetic and copies ran while one was open for 1% of the time, Pallas kernels for 2%

profile of v1, /device:TPU:1, one launch (start us, length us, event | category | flops | bytes accessed | tf_op | source)
XLA Modules:
  0.0 137.3 jit_solution(11649327507068841422)
XLA Ops:
  0.7 1.1 concatenate.10
  1.8 4.4 %collective-permute-start = (f32[8,1024]{1,0:T(8,128)S(1)}, f32[8,1024]{1,0:T(8,128)S(1)}, u32[]{:S(2)}, u32[]{:S(2)}) collective-permute-start(f32[8,1024]{1,0:T(8,128)S(1)} %get-tuple-element.10), channel_id=1, source_target_pairs={{0,8},{8,16},{16,24},{24,32},{32,40},{40,48},{48,56},{56,64},{64,7... | collective-permute-start | bytes 98312 | tf_op jit(solution)/shard_map/ppermute | solution.py:162
  6.2 1.3 collective-permute-start.1
  7.5 0.7 add_convert_fusion
  8.2 0.1 copy.16
  8.4 0.0 copy-start
  8.4 0.9 copy-done
  9.3 0.0 copy-start.1
  9.3 0.9 copy-done.1
  10.2 0.0 copy-start.2
  10.2 0.7 copy-done.2
  10.9 3.2 %pack.1 = (f32[2048,128]{1,0:T(8,128)}, s32[256]{0:T(256)S(1)}) custom-call(s32[256]{0:T(256)S(1)} %bitcast.11, f32[2,32768]{1,0:T(2,128)S(1)} %copy-done, f32[256,128]{1,0:T(8,128)S(1)} %bitcast.10, f32[256,128]{1,0:T(8,128)S(1)} %pad.4.labels), custom_call_target="tpu_custom_call" | custom-call | tf_op jit(solution)/shard_map/pack/pallas_call | solution.py:142
  14.2 11.7 %all-to-all-start = ((f32[128,16,128]{2,1,0:T(8,128)}), f32[128,16,128]{2,1,0:T(8,128)S(1)}, u32[]{:S(2)}, u32[]{:S(2)}) async-start(f32[128,16,128]{2,1,0:T(8,128)} %bitcast.2), calls=%async_computation | async-start | bytes 2097152 | tf_op jit(solution)/shard_map/all_to_all | solution.py:154
  25.8 0.0 collective-permute-done
  25.9 0.0 collective-permute-done.1
  25.9 19.0 %all-to-all-done = f32[128,16,128]{2,1,0:T(8,128)S(1)} async-done(((f32[128,16,128]{2,1,0:T(8,128)}), f32[128,16,128]{2,1,0:T(8,128)S(1)}, u32[]{:S(2)}, u32[]{:S(2)}) %all-to-all-start) | async-done | bytes 1048608 | tf_op jit(solution)/shard_map/all_to_all | solution.py:154
  44.9 0.1 slice_convert_fusion
  45.0 0.3 reshape.28.labels
  45.3 38.4 %match.1 = f32[128,24,128]{2,1,0:T(8,128)S(1)} custom-call(s32[2560]{0:T(1024)S(1)} %reshape.28.labels, f32[2048,128]{1,0:T(8,128)S(1)} %bitcast.9, f32[8,10240]{1,0:T(8,128)S(1)} %pad_maximum_fusion.window), custom_call_target="tpu_custom_call" | custom-call | tf_op jit(solution)/shard_map/match/pallas_call | solution.py:167
  83.7 49.8 %all_to_all.10 = f32[128,24,128]{2,1,0:T(8,128)S(1)} all-to-all(f32[128,24,128]{2,1,0:T(8,128)S(1)} %match.1), channel_id=1, replica_groups=mesh['zone'=16,'tile'=8] {'zone','tile'}, dimensions={0} | all-to-all | bytes 3145728 | tf_op jit(solution)/shard_map/all_to_all | solution.py:180
  133.4 3.9 %unpack.1 = (f32[5,32768]{1,0:T(8,128)}, f32[256,128]{1,0:T(8,128)}) custom-call(s32[256]{0:T(256)S(1)} %get-tuple-element.6.place, f32[3072,128]{1,0:T(8,128)S(1)} %bitcast.8), custom_call_target="tpu_custom_call" | custom-call | tf_op jit(solution)/shard_map/unpack/pallas_call | solution.py:181
  (4 shorter events, 0.1 us)
Async XLA Ops:
  1.8 24.0 %collective-permute-start = (f32[8,1024]{1,0:T(8,128)S(1)}, f32[8,1024]{1,0:T(8,128)S(1)}, u32[]{:S(2)}, u32[]{:S(2)}) collective-permute-start(f32[8,1024]{1,0:T(8,128)S(1)} %get-tuple-element.10), channel_id=1, source_target_pairs={{0,8},{8,16},{16,24},{24,32},{32,40},{40,48},{48,56},{56,64},{64,7... | collective-permute-start | bytes 98312 | tf_op jit(solution)/shard_map/ppermute | solution.py:162
  6.2 19.7 %collective-permute-start.1 = (f32[8,1024]{1,0:T(8,128)S(1)}, f32[8,1024]{1,0:T(8,128)S(1)}, u32[]{:S(2)}, u32[]{:S(2)}) collective-permute-start(f32[8,1024]{1,0:T(8,128)S(1)} %get-tuple-element.11), channel_id=1, source_target_pairs={{8,0},{16,8},{24,16},{32,24},{40,32},{48,40},{56,48},{64,56},{72,6... | collective-permute-start | bytes 98312 | tf_op jit(solution)/shard_map/ppermute | solution.py:163
  8.4 1.0 copy-start
  9.3 0.9 copy-start.1
  10.2 0.7 copy-start.2
  14.2 30.8 %all-to-all-start = ((f32[128,16,128]{2,1,0:T(8,128)}), f32[128,16,128]{2,1,0:T(8,128)S(1)}, u32[]{:S(2)}, u32[]{:S(2)}) async-start(f32[128,16,128]{2,1,0:T(8,128)} %bitcast.2), calls=%async_computation | async-start | bytes 2097152 | tf_op jit(solution)/shard_map/all_to_all | solution.py:154

commit v2 on v1

--- a/solution.py
+++ b/solution.py
@@ -12,7 +12,10 @@
 K = 4
 MB = 8
 CAP = 4
-UNROLL = 16
+UNROLL = 20
+GROUP = 2
+TERMS = 24
+DEAD = 127
 SCALE = math.sqrt(0.5 / math.log(2.0))
 F32 = jnp.float32
 BF16 = jnp.bfloat16
@@ -44,62 +47,171 @@
     lax.fori_loop(0, dest.shape[0], one, 0, unroll=4)
 
 
-def match_kernel(labels, a_rows, window, out, wide, acc, todo):
-    slots = a_rows.shape[0] // 4
-    messages = slots // CAP
-    blocks = window.shape[1] // TB
-    steps = 16
+def split(x):
+    first = x.astype(BF16).astype(F32)
+    second = (x - first).astype(BF16).astype(F32)
+    return first, second, x - first - second
+
+
+def left_terms(tile):
+    u, v = tile[0:1] * SCALE, tile[1:2] * SCALE
+    u, v, n = split(u), split(v), split(u * u + v * v)
+    one = jnp.ones_like(u[0])
+    rows = [u[0], v[0], u[0], v[0], u[0], v[0], one, one]
+    rows += [u[1], v[1], u[1], v[1], u[2], v[2], one, n[0], n[1], n[2]]
+    return jnp.concatenate(rows + [jnp.zeros((TB - len(rows), TB), F32)], axis=0)
+
+
+def right_terms(a_rows, right, g):
+    for r in range(CAP):
+        u, v = (a_rows[pl.ds(g * 128 + 4 * q + r, 8, stride=16), :] * SCALE for q in range(2))
+        n = split(u * u + v * v)
+        u, v = split(-2.0 * u), split(-2.0 * v)
+        one = jnp.ones_like(u[0])
+        rows = [u[0], v[0], u[1], v[1], u[2], v[2], n[0], n[1]]
+        rows += [u[0], v[0], u[1], v[1], u[0], v[0], n[2], one]
+        rows += [one] * (TERMS - len(rows))
+        for k, x in enumerate(rows):
+            right[pl.ds((g * 8 * CAP + r) * TERMS + k, 8, stride=CAP * TERMS), :] = x
+
+
+def sort_pairs(a_rows, order, codes):
+    messages = a_rows.shape[0] // 16
+    line = lax.broadcasted_iota(jnp.int32, (TB, messages), 0).astype(F32)
+    lane = lax.broadcasted_iota(jnp.int32, (1, messages), 1)
+    keys = [None] * 16
+    for r in range(CAP):
+        turned = a_rows[pl.ds(12 + r, messages, stride=16), :].T
+        for k in range(K):
+            keys[4 * k + r] = jnp.where(turned[K : K + 1] > k, turned[k : k + 1], float(DEAD))
+    marks = [(line == key).astype(F32) for key in keys]
+    here = functools.reduce(jnp.add, marks)
+    before = lax.broadcasted_iota(jnp.int32, (TB, TB), 0) < lax.broadcasted_iota(jnp.int32, (TB, TB), 1)
+    before = before.astype(F32)
+    after = before.T.astype(BF16)
+    both = jnp.concatenate([before, jnp.ones_like(before)], axis=1).astype(BF16)
+    sums = jnp.dot(here.astype(BF16), both, preferred_element_type=F32)
+    groups = jnp.floor((sums[:, TB:] + (GROUP - 1)) * (1.0 / GROUP))
+    coarse = jnp.floor(groups * (1.0 / 16))
+    first = 16.0 * jnp.dot(after, coarse.astype(BF16), preferred_element_type=F32)
+    first = first + jnp.dot(after, (groups - 16.0 * coarse).astype(BF16), preferred_element_type=F32)
+    place = sums[:, :TB] + GROUP * first
+    for row in range(16):
+        spot = jnp.sum(marks[row] * place, axis=0, keepdims=True)
+        live = keys[row] < DEAD
+        order[row : row + 1, :] = jnp.where(live, spot, float(order_dump(messages))).astype(jnp.int32)
+        codes[row : row + 1, :] = (lane * CAP + row % 4) * TB + keys[row].astype(jnp.int32)
+        if row < 15:
+            place = place + marks[row]
+    order[16:17, :] = first[DEAD : DEAD + 1].astype(jnp.int32)
+
+
+def order_dump(messages):
+    return messages * CAP * K + 80 * (GROUP - 1) + GROUP * UNROLL
+
+
+def list_size(messages):
+    return order_dump(messages) + 1
+
+
+def prepare_kernel(window, wide, left):
+    def one(w, c):
+        tile = window[:, pl.ds(pl.multiple_of(w * TB, TB), TB)]
+        wide[w] = jnp.broadcast_to(-tile[5:6], (TB, TB)).T
+        left[w] = left_terms(tile).T.astype(BF16)
+        return c
+
+    lax.fori_loop(0, wide.shape[0], one, 0, unroll=4)
+
+
+def match_kernel(a_rows, window, wide_far, left_far, out, wide, left, right, acc, order, codes, blank, order_s, codes_s, todo, sems):
+    messages = a_rows.shape[0] // 16
+    slots = messages * CAP
     row = lax.broadcasted_iota(jnp.int32, (8, TB), 0)
+    fetches = [
+        pltpu.make_async_copy(wide_far, wide, sems.at[3]),
+        pltpu.make_async_copy(left_far, left, sems.at[4]),
+    ]
+    for fetch in fetches:
+        fetch.start()
+    sort_pairs(a_rows, order, codes)
+    blank[...] = jnp.full(blank.shape, slots * TB, jnp.int32)
+    copies = [
+        pltpu.make_async_copy(order, order_s, sems.at[0]),
+        pltpu.make_async_copy(codes, codes_s, sems.at[1]),
+        pltpu.make_async_copy(blank, todo, sems.at[2]),
+    ]
+    for copy in copies:
+        copy.start()
     acc[...] = jnp.zeros_like(acc)
 
-    def prepare(step, n):
-        for k in range(blocks // steps):
-            w = step * (blocks // steps) + k
-            tile = window[:, pl.ds(pl.multiple_of(w * TB, TB), TB)]
-            for q, line, gain in ((0, 0, SCALE), (1, 1, SCALE), (2, 5, 1.0)):
-                wide[w, q] = jnp.broadcast_to(tile[line : line + 1] * gain, (TB, TB)).T
-        for k in range(messages // steps * CAP):
-            slot = step * (messages // steps * CAP) + k
-            for p in range(K):
-                todo[n + p] = slot * TB + labels[slot * 5 + p]
-            n = n + labels[slot * 5 + K]
-        return n
-
-    pairs = lax.fori_loop(0, steps, prepare, 0)
-    for k in range(UNROLL):
-        todo[pairs + k] = slots * TB
-
-    def pair(code):
-        slot = jnp.minimum(code // TB, slots - 1)
-        w = code % TB
-        base = slot // CAP * 16 + slot % CAP
+    def turn(g, c):
+        right_terms(a_rows, right, g)
+        return c
+
+    lax.fori_loop(0, messages // 8, turn, 0)
+    for copy in copies:
+        copy.wait()
+
+    def put(m, c):
+        for e in range(16):
+            p = order_s[e, m]
+            todo[p] = codes_s[e, m]
+        return c
+
+    lax.fori_loop(0, messages, put, 0, unroll=2)
+    for fetch in fetches:
+        fetch.wait()
+    groups = order_s[16, 0]
+
+    def group(code):
+        w = code[0] & (TB - 1)
+        slot = [jnp.minimum(lax.shift_right_logical(c, 7), slots - 1) for c in code]
+        base = [lax.shift_right_logical(s, 2) * 16 + (s & 3) for s in slot]
         tile = window[:, pl.ds(pl.multiple_of(w * TB, TB), TB)]
-        du = wide[w, 0] - a_rows[pl.ds(base, 1), :] * SCALE
-        dv = wide[w, 1] - a_rows[pl.ds(base + 4, 1), :] * SCALE
-        r = pltpu.reciprocal(wide[w, 2] + a_rows[pl.ds(base + 8, 1), :], approx=True)
-        weight = r * jnp.exp2((du * du + dv * dv) * -r)
-        q = jnp.where(row == 5, 2.0, 2.0 * tile) * tile[6:7]
+
+        spare = jnp.zeros((32 - TERMS, TB), F32)
+        terms = [
+            jnp.concatenate([right[pl.ds(pl.multiple_of(t * TERMS, 8), TERMS), :], spare], axis=0)
+            for t in slot
+        ]
+        terms = jnp.concatenate(terms, axis=1).astype(BF16)
+        apart = jnp.dot(left[w][:, :32], terms, preferred_element_type=F32)
+        spread = [jnp.broadcast_to(a_rows[pl.ds(b + 8, 1), :], (8, TB)) for b in base]
+        high, low = [[] for _ in code], [[] for _ in code]
+        for strip in range(0, TB, 16):
+            s = [wide[w, strip + h : strip + h + 8, :] for h in (0, 8)]
+            for e in range(GROUP):
+                weight = []
+                for h in range(2):
+                    d2 = apart[strip + 8 * h : strip + 8 * h + 8, e * TB : (e + 1) * TB]
+                    r = pltpu.reciprocal(s[h] - spread[e], approx=True)
+                    weight.append(r * jnp.exp2(d2 * r))
+                weight = jnp.concatenate(weight, axis=0)
+                high[e].append(weight.astype(BF16))
+                low[e].append((weight - high[e][-1].astype(F32)).astype(BF16))
+        q = jnp.where(row == 5, -2.0, -2.0 * tile) * tile[6:7]
         q_high = q.astype(BF16).astype(F32)
         q = jnp.concatenate([q_high, q - q_high], axis=0).astype(BF16)
-        high = weight.astype(BF16)
-        low = (weight - high.astype(F32)).astype(BF16)
-        total = jnp.dot(
-            jnp.concatenate([q, q], axis=1),
-            jnp.concatenate([high, low], axis=0),
-            preferred_element_type=F32,
-        )
-        return total[0:8] + total[8:16]
+        q = jnp.concatenate([q, q], axis=1)
+        total = []
+        for e in range(GROUP):
+            t = jnp.dot(q, jnp.concatenate(high[e] + low[e], axis=0), preferred_element_type=F32)
+            total.append(t[0:8] + t[8:16])
+        return total
 
     def chunk(c, carry):
         done = []
         for k in range(UNROLL):
-            code = todo[c * UNROLL + k]
-            done.append((code // TB, pair(code)))
-        for slot, total in done:
-            acc[slot] = acc[slot] + total
+            code = [todo[(c * UNROLL + k) * GROUP + e] for e in range(GROUP)]
+            done.append((code, group(code)))
+        for code, total in done:
+            for e in range(GROUP):
+                slot = lax.shift_right_logical(code[e], 7)
+                acc[slot] = acc[slot] + total[e]
         return carry
 
-    lax.fori_loop(0, (pairs + UNROLL - 1) // UNROLL, chunk, 0)
+    lax.fori_loop(0, (groups + UNROLL - 1) // UNROLL, chunk, 0)
 
     def finish(m, carry):
         parts = []
@@ -126,11 +238,54 @@
 
 
 VMEM = pl.BlockSpec(memory_space=pltpu.VMEM)
+FAR = pl.BlockSpec(memory_space=pl.ANY)
 SMEM = pl.BlockSpec(memory_space=pltpu.SMEM)
 
 
 def params(mib):
     return pltpu.CompilerParams(vmem_limit_bytes=mib * 2**20)
+
+
+def prepare_call(window):
+    blocks = window.shape[1] // TB
+    return pl.pallas_call(
+        prepare_kernel,
+        out_shape=(
+            jax.ShapeDtypeStruct((blocks, TB, TB), F32),
+            jax.ShapeDtypeStruct((blocks, TB, TB), BF16),
+        ),
+        in_specs=[VMEM],
+        out_specs=(VMEM, VMEM),
+        compiler_params=params(16),
+        cost_estimate=pl.CostEstimate(flops=10**8, bytes_accessed=10**7, transcendentals=0),
+        name="prepare",
+    )(window)
+
+
+def match_call(a_rows, window, wide, left):
+    messages = a_rows.shape[0] // 16
+    size = -(-list_size(messages) // 1024) * 1024
+    return pl.pallas_call(
+        match_kernel,
+        out_shape=jax.ShapeDtypeStruct((messages, CAP * 6, TB), F32),
+        in_specs=[VMEM, VMEM, FAR, FAR],
+        out_specs=VMEM,
+        scratch_shapes=[
+            pltpu.VMEM(wide.shape, wide.dtype),
+            pltpu.VMEM(left.shape, left.dtype),
+            pltpu.VMEM((messages * CAP * TERMS, TB), F32),
+            pltpu.VMEM((messages * CAP + 1, 8, TB), F32),
+            pltpu.VMEM((24, messages), jnp.int32),
+            pltpu.VMEM((16, messages), jnp.int32),
+            pltpu.VMEM((size,), jnp.int32),
+            pltpu.SMEM((24, messages), jnp.int32),
+            pltpu.SMEM((16, messages), jnp.int32),
+            pltpu.SMEM((size,), jnp.int32),
+            pltpu.SemaphoreType.DMA((5,)),
+        ],
+        compiler_params=params(28),
+        name="match",
+    )(a_rows, window, wide, left)
 
 
 def body(a_coord, a_var, dest, cand, cand_count, b_coord, b_var, b_prior, b_flux):
@@ -151,6 +306,9 @@
         compiler_params=params(16),
         name="pack",
     )(dest.reshape(count), a_coord, a_var.reshape(count, TB), labels)
+    send, b_coord, b_flux, b_var, b_prior = lax.optimization_barrier(
+        (send, b_coord, b_flux, b_var, b_prior)
+    )
     got = lax.all_to_all(
         send.reshape(devices, 16, TB), ("zone", "tile"), split_axis=0, concat_axis=0, tiled=True
     )
@@ -162,21 +320,8 @@
     below = lax.ppermute(own[:, -width:], "zone", up)
     above = lax.ppermute(own[:, :width], "zone", [(j, i) for i, j in up])
     window = jnp.concatenate([below, own, above], axis=1)
-    got_labels = got[:, 12:16, : K + 1].astype(jnp.int32).reshape(-1)
     slots = devices * CAP
-    result = pl.pallas_call(
-        match_kernel,
-        out_shape=jax.ShapeDtypeStruct((devices, CAP * 6, TB), F32),
-        in_specs=[SMEM, VMEM, VMEM],
-        out_specs=VMEM,
-        scratch_shapes=[
-            pltpu.VMEM((window.shape[1] // TB, 3, TB, TB), F32),
-            pltpu.VMEM((slots + 1, 8, TB), F32),
-            pltpu.SMEM((slots * K + UNROLL + K,), jnp.int32),
-        ],
-        compiler_params=params(40),
-        name="match",
-    )(got_labels, got.reshape(devices * 16, TB), window)
+    result = match_call(got.reshape(devices * 16, TB), window, *prepare_call(window))
     back = lax.all_to_all(result, ("zone", "tile"), split_axis=0, concat_axis=0, tiled=True)
     matched, prob = pl.pallas_call(
         unpack_kernel,

time: 138 us -> 125 us (0.906)
  local copies, waits for them, and re-layouts: 4.12 us -> 11.8 us
  waiting for transfers between devices: 19 us -> 11.5 us
  Pallas kernels: 45.5 us -> 38.3 us
  blocking collectives: 49.8 us -> 44.1 us
    unnamed x6 -> x14, local copies, waits for them, and re-layouts: 2.53 us -> 10.5 us
    all_to_all x1, waiting for transfers between devices: 19 us -> 11.5 us  [body(): lax.all_to_all(send.reshape(devices, 16, TB), ('zone', 'tile'), split_axi...]
    pallas_call x1 -> x2, Pallas kernels: 38.4 us -> 31.2 us  [the longest x1 27.5 us: match_call(): pl.pallas_call(match_kernel, out_shape=jax.ShapeDtypeStruct((messages, CA...]
    all_to_all x1, blocking collectives: 49.8 us -> 44.1 us  [body(): lax.all_to_all(result, ('zone', 'tile'), split_axis=0, concat_axis=0, til...]
  transfers between devices with their start and end apart: 3 -> 3, of which waited for: 1 -> 1; matrix products, arithmetic and copies ran while one was open for 1% -> 0% of each run, Pallas kernels for 2% -> 3%
where the time goes in v2:
time: 125 us
  blocking collectives  44.1 us (35%)
  Pallas kernels  38.3 us (31%)
  starting transfers between devices  17.3 us (14%)
  local copies, waits for them, and re-layouts  11.8 us (9%)
  waiting for transfers between devices  11.5 us (9%)
    all_to_all x1, blocking collectives, body(): lax.all_to_all(result, ('zone', 'tile'), split_axis=0, concat_axis=0, til...  44.1 us
    pallas_call x1, Pallas kernels, match_call(): pl.pallas_call(match_kernel, out_shape=jax.ShapeDtypeStruct((messages, CA...  27.5 us
    all_to_all x1, starting transfers between devices, body(): lax.all_to_all(send.reshape(devices, 16, TB), ('zone', 'tile'), split_axi...  11.7 us
    all_to_all x1, waiting for transfers between devices, body(): lax.all_to_all(send.reshape(devices, 16, TB), ('zone', 'tile'), split_axi...  11.5 us
    unnamed x14, local copies, waits for them, and re-layouts  10.5 us
    ppermute x1, starting transfers between devices, body(): below = lax.ppermute(own[:, -width:], 'zone', up)  4.37 us
    pallas_call x1, Pallas kernels, body(): pl.pallas_call(unpack_kernel, out_shape=(jax.ShapeDtypeStruct((5, count *...  3.87 us
    pallas_call x1, Pallas kernels, prepare_call(): pl.pallas_call(prepare_kernel, out_shape=(jax.ShapeDtypeStruct((blocks, T...  3.69 us
  transfers between devices with their start and end apart: 3, of which 1 were waited for; matrix products, arithmetic and copies ran while one was open for 0% of the time, Pallas kernels for 3%

profile of v2, /device:TPU:1, one launch (start us, length us, event | category | flops | bytes accessed | tf_op | source)
XLA Modules:
  0.0 124.6 jit_solution(8318183961522273529)
XLA Ops:
  0.6 0.7 add_convert_fusion
  1.3 0.1 copy.14
  1.5 0.0 copy-start.4
  1.5 0.9 copy-done.4
  2.5 0.0 copy-start.5
  2.5 0.9 copy-done.5
  3.4 0.0 copy-start.6
  3.4 0.7 copy-done.6
  4.0 3.2 %pack.1 = (f32[2048,128]{1,0:T(8,128)}, s32[256]{0:T(256)S(1)}) custom-call(s32[256]{0:T(256)S(1)} %bitcast.11, f32[2,32768]{1,0:T(2,128)S(1)} %copy-done.4, f32[256,128]{1,0:T(8,128)S(1)} %bitcast.10, f32[256,128]{1,0:T(8,128)S(1)} %pad.4.labels), custom_call_target="tpu_custom_call" | custom-call | tf_op jit(solution)/shard_map/pack/pallas_call | solution.py:297
  7.3 1.1 concatenate.10
  8.5 4.4 %collective-permute-start = (f32[8,1024]{1,0:T(8,128)S(1)}, f32[8,1024]{1,0:T(8,128)S(1)}, u32[]{:S(2)}, u32[]{:S(2)}) collective-permute-start(f32[8,1024]{1,0:T(8,128)S(1)} %get-tuple-element.24), channel_id=1, source_target_pairs={{0,8},{8,16},{16,24},{24,32},{32,40},{40,48},{48,56},{56,64},{64,7... | collective-permute-start | bytes 98312 | tf_op jit(solution)/shard_map/ppermute | solution.py:320
  12.9 1.3 %collective-permute-start.1 = (f32[8,1024]{1,0:T(8,128)S(1)}, f32[8,1024]{1,0:T(8,128)S(1)}, u32[]{:S(2)}, u32[]{:S(2)}) collective-permute-start(f32[8,1024]{1,0:T(8,128)S(1)} %get-tuple-element.25), channel_id=1, source_target_pairs={{8,0},{16,8},{24,16},{32,24},{40,32},{48,40},{56,48},{64,56},{72,6... | collective-permute-start | bytes 98312 | tf_op jit(solution)/shard_map/ppermute | solution.py:321
  14.2 11.7 %all-to-all-start = ((f32[128,16,128]{2,1,0:T(8,128)}), f32[128,16,128]{2,1,0:T(8,128)S(1)}, u32[]{:S(2)}, u32[]{:S(2)}) async-start(f32[128,16,128]{2,1,0:T(8,128)} %bitcast.2), calls=%async_computation | async-start | bytes 2097152 | tf_op jit(solution)/shard_map/all_to_all | solution.py:312
  25.8 0.0 collective-permute-done
  25.9 0.0 collective-permute-done.1
  25.9 3.7 %prepare.1 = (f32[80,128,128]{2,1,0:T(8,128)S(1)}, bf16[80,128,128]{2,1,0:T(8,128)(2,1)S(1)}) custom-call(f32[8,10240]{1,0:T(8,128)S(1)} %pad_maximum_fusion.window), custom_call_target="tpu_custom_call" | custom-call | flops 100000000 | bytes 10000000 | tf_op jit(solution)/shard_map/prepare/pallas_call | solution.py:251
  29.6 0.0 copy-start
  29.6 2.3 %copy-done = f32[80,128,128]{2,1,0:T(8,128)} copy-done((f32[80,128,128]{2,1,0:T(8,128)}, f32[80,128,128]{2,1,0:T(8,128)S(1)}, u32[]{:S(2)}) %copy-start) | copy-done | bytes 5242904
  31.9 0.0 copy-start.2
  31.9 1.5 %copy-done.2 = bf16[80,128,128]{2,1,0:T(8,128)(2,1)} copy-done((bf16[80,128,128]{2,1,0:T(8,128)(2,1)}, bf16[80,128,128]{2,1,0:T(8,128)(2,1)S(1)}, u32[]{:S(2)}) %copy-start.2) | copy-done | bytes 2621464
  33.4 11.5 %all-to-all-done = f32[128,16,128]{2,1,0:T(8,128)S(1)} async-done(((f32[128,16,128]{2,1,0:T(8,128)}), f32[128,16,128]{2,1,0:T(8,128)S(1)}, u32[]{:S(2)}, u32[]{:S(2)}) %all-to-all-start) | async-done | bytes 1048608 | tf_op jit(solution)/shard_map/all_to_all | solution.py:312
  44.9 0.0 copy-start.1
  44.9 2.5 %copy-done.1 = f32[80,128,128]{2,1,0:T(8,128)S(1)} copy-done((f32[80,128,128]{2,1,0:T(8,128)S(1)}, f32[80,128,128]{2,1,0:T(8,128)}, u32[]{:S(2)}) %copy-start.1) | copy-done | bytes 5242904
  47.4 0.0 copy-start.3
  47.4 1.7 %copy-done.3 = bf16[80,128,128]{2,1,0:T(8,128)(2,1)S(1)} copy-done((bf16[80,128,128]{2,1,0:T(8,128)(2,1)S(1)}, bf16[80,128,128]{2,1,0:T(8,128)(2,1)}, u32[]{:S(2)}) %copy-start.3) | copy-done | bytes 2621464
  49.1 27.5 %match.1 = f32[128,24,128]{2,1,0:T(8,128)S(1)} custom-call(f32[2048,128]{1,0:T(8,128)S(1)} %bitcast.9, f32[8,10240]{1,0:T(8,128)S(1)} %pad_maximum_fusion.window, f32[80,128,128]{2,1,0:T(8,128)S(1)} %copy-done.1, bf16[80,128,128]{2,1,0:T(8,128)(2,1)S(1)} %copy-done.3), custom_call_target="tpu_custom_call" | custom-call | tf_op jit(solution)/shard_map/match/pallas_call | solution.py:268
  76.6 44.1 %all_to_all.10 = f32[128,24,128]{2,1,0:T(8,128)S(1)} all-to-all(f32[128,24,128]{2,1,0:T(8,128)S(1)} %match.1), channel_id=1, replica_groups=mesh['zone'=16,'tile'=8] {'zone','tile'}, dimensions={0} | all-to-all | bytes 3145728 | tf_op jit(solution)/shard_map/all_to_all | solution.py:325
  120.7 3.9 %unpack.1 = (f32[5,32768]{1,0:T(8,128)}, f32[256,128]{1,0:T(8,128)}) custom-call(s32[256]{0:T(256)S(1)} %get-tuple-element.13.place, f32[3072,128]{1,0:T(8,128)S(1)} %bitcast.8), custom_call_target="tpu_custom_call" | custom-call | tf_op jit(solution)/shard_map/unpack/pallas_call | solution.py:326
  (4 shorter events, 0.1 us)
Async XLA Ops:
  1.5 1.0 copy-start.4
  2.5 0.9 copy-start.5
  3.4 0.7 copy-start.6
  8.5 17.4 %collective-permute-start = (f32[8,1024]{1,0:T(8,128)S(1)}, f32[8,1024]{1,0:T(8,128)S(1)}, u32[]{:S(2)}, u32[]{:S(2)}) collective-permute-start(f32[8,1024]{1,0:T(8,128)S(1)} %get-tuple-element.24), channel_id=1, source_target_pairs={{0,8},{8,16},{16,24},{24,32},{32,40},{40,48},{48,56},{56,64},{64,7... | collective-permute-start | bytes 98312 | tf_op jit(solution)/shard_map/ppermute | solution.py:320
  12.9 13.0 %collective-permute-start.1 = (f32[8,1024]{1,0:T(8,128)S(1)}, f32[8,1024]{1,0:T(8,128)S(1)}, u32[]{:S(2)}, u32[]{:S(2)}) collective-permute-start(f32[8,1024]{1,0:T(8,128)S(1)} %get-tuple-element.25), channel_id=1, source_target_pairs={{8,0},{16,8},{24,16},{32,24},{40,32},{48,40},{56,48},{64,56},{72,6... | collective-permute-start | bytes 98312 | tf_op jit(solution)/shard_map/ppermute | solution.py:321
  14.2 30.8 %all-to-all-start = ((f32[128,16,128]{2,1,0:T(8,128)}), f32[128,16,128]{2,1,0:T(8,128)S(1)}, u32[]{:S(2)}, u32[]{:S(2)}) async-start(f32[128,16,128]{2,1,0:T(8,128)} %bitcast.2), calls=%async_computation | async-start | bytes 2097152 | tf_op jit(solution)/shard_map/all_to_all | solution.py:312
  29.6 2.3 %copy-start = (f32[80,128,128]{2,1,0:T(8,128)}, f32[80,128,128]{2,1,0:T(8,128)S(1)}, u32[]{:S(2)}) copy-start(f32[80,128,128]{2,1,0:T(8,128)S(1)} %get-tuple-element.20.wide_far) | copy-start | bytes 15728644
  31.9 1.5 %copy-start.2 = (bf16[80,128,128]{2,1,0:T(8,128)(2,1)}, bf16[80,128,128]{2,1,0:T(8,128)(2,1)S(1)}, u32[]{:S(2)}) copy-start(bf16[80,128,128]{2,1,0:T(8,128)(2,1)S(1)} %get-tuple-element.21.left_far) | copy-start | bytes 7864324
  44.9 2.5 %copy-start.1 = (f32[80,128,128]{2,1,0:T(8,128)S(1)}, f32[80,128,128]{2,1,0:T(8,128)}, u32[]{:S(2)}) copy-start(f32[80,128,128]{2,1,0:T(8,128)} %copy-done) | copy-start | bytes 15728644
  47.4 1.7 %copy-start.3 = (bf16[80,128,128]{2,1,0:T(8,128)(2,1)S(1)}, bf16[80,128,128]{2,1,0:T(8,128)(2,1)}, u32[]{:S(2)}) copy-start(bf16[80,128,128]{2,1,0:T(8,128)(2,1)} %copy-done.2) | copy-start | bytes 7864324

commit v3 on v2

--- a/solution.py
+++ b/solution.py
@@ -14,15 +14,21 @@
 CAP = 4
 UNROLL = 20
 GROUP = 2
-TERMS = 24
+TERMS = 32
 DEAD = 127
 SCALE = math.sqrt(0.5 / math.log(2.0))
 F32 = jnp.float32
 BF16 = jnp.bfloat16
 
 
-def pack_kernel(dest, a_coord, a_var, labels, send, place, taken):
+def pack_kernel(dest, far_coord, far_var, labels, send, place, taken, a_coord, a_var, sems):
     devices = taken.shape[0]
+    fetches = [
+        pltpu.make_async_copy(far_coord, a_coord, sems.at[0]),
+        pltpu.make_async_copy(far_var, a_var, sems.at[1]),
+    ]
+    for fetch in fetches:
+        fetch.start()
     send[...] = jnp.zeros_like(send)
 
     def clear(i, c):
@@ -30,21 +36,23 @@
         return c
 
     lax.fori_loop(0, devices, clear, 0, unroll=8)
+    for fetch in fetches:
+        fetch.wait()
 
     def one(b, c):
         d = dest[b]
         r = taken[d]
         taken[d] = r + 1
-        place[b] = d * 4 + r
-        row = d * 16 + r
+        place[b] = d * (CAP * 6) + r * 6
+        row = d * 16 + r * 4
         lanes = pl.ds(pl.multiple_of(b * TB, TB), TB)
         send[pl.ds(row, 1), :] = a_coord[0:1, lanes]
-        send[pl.ds(row + 4, 1), :] = a_coord[1:2, lanes]
-        send[pl.ds(row + 8, 1), :] = a_var[pl.ds(b, 1), :]
-        send[pl.ds(row + 12, 1), :] = labels[pl.ds(b, 1), :]
-        return c
-
-    lax.fori_loop(0, dest.shape[0], one, 0, unroll=4)
+        send[pl.ds(row + 1, 1), :] = a_coord[1:2, lanes]
+        send[pl.ds(row + 2, 1), :] = a_var[pl.ds(b, 1), :]
+        send[pl.ds(row + 3, 1), :] = labels[pl.ds(b, 1), :]
+        return c
+
+    lax.fori_loop(0, dest.shape[0], one, 0, unroll=8)
 
 
 def split(x):
@@ -57,22 +65,27 @@
     u, v = tile[0:1] * SCALE, tile[1:2] * SCALE
     u, v, n = split(u), split(v), split(u * u + v * v)
     one = jnp.ones_like(u[0])
-    rows = [u[0], v[0], u[0], v[0], u[0], v[0], one, one]
-    rows += [u[1], v[1], u[1], v[1], u[2], v[2], one, n[0], n[1], n[2]]
+    zero = jnp.zeros_like(one)
+    rows = [u[0], v[0], one, n[0], u[0], v[0], one, zero, u[0], v[0], one, zero]
+    rows += [u[1], v[1], zero, n[1], u[1], v[1], zero, zero, u[2], v[2], zero, n[2]]
     return jnp.concatenate(rows + [jnp.zeros((TB - len(rows), TB), F32)], axis=0)
 
 
-def right_terms(a_rows, right, g):
-    for r in range(CAP):
-        u, v = (a_rows[pl.ds(g * 128 + 4 * q + r, 8, stride=16), :] * SCALE for q in range(2))
-        n = split(u * u + v * v)
-        u, v = split(-2.0 * u), split(-2.0 * v)
-        one = jnp.ones_like(u[0])
-        rows = [u[0], v[0], u[1], v[1], u[2], v[2], n[0], n[1]]
-        rows += [u[0], v[0], u[1], v[1], u[0], v[0], n[2], one]
-        rows += [one] * (TERMS - len(rows))
-        for k, x in enumerate(rows):
-            right[pl.ds((g * 8 * CAP + r) * TERMS + k, 8, stride=CAP * TERMS), :] = x
+def right_terms(a_rows, right, m):
+    row = lax.broadcasted_iota(jnp.int32, (8, TB), 0)
+    upper, kind = row < 4, row & 3
+    for half in range(CAP // 2):
+        tile = a_rows[pl.ds(pl.multiple_of(m * 16 + 8 * half, 8), 8), :] * SCALE
+        square = tile * tile
+        square = pltpu.roll(square, 1, 0) + pltpu.roll(square, 2, 0)
+        y = split(jnp.where(kind < 2, -2.0 * tile, jnp.where(kind == 2, square, 1.0)))
+        z = [pltpu.roll(x, 4, 0) for x in y]
+        for odd in range(2):
+            y, z = (z, y) if odd else (y, z)
+            parts = [jnp.where(upper, y[i], z[j]) for i, j in ((0, 1), (2, 0), (1, 0))]
+            parts = jnp.concatenate(parts + [jnp.zeros((8, TB), F32)], axis=0)
+            start = (m * CAP + 2 * half + odd) * TERMS
+            right[pl.ds(pl.multiple_of(start, TERMS), TERMS), :] = parts.astype(BF16)
 
 
 def sort_pairs(a_rows, order, codes):
@@ -81,7 +94,7 @@
     lane = lax.broadcasted_iota(jnp.int32, (1, messages), 1)
     keys = [None] * 16
     for r in range(CAP):
-        turned = a_rows[pl.ds(12 + r, messages, stride=16), :].T
+        turned = a_rows[pl.ds(4 * r + 3, messages, stride=16), :].T
         for k in range(K):
             keys[4 * k + r] = jnp.where(turned[K : K + 1] > k, turned[k : k + 1], float(DEAD))
     marks = [(line == key).astype(F32) for key in keys]
@@ -124,14 +137,23 @@
     lax.fori_loop(0, wide.shape[0], one, 0, unroll=4)
 
 
-def match_kernel(a_rows, window, wide_far, left_far, out, wide, left, right, acc, order, codes, blank, order_s, codes_s, todo, sems):
+def match_kernel(
+    a_rows, own, below, above, wide_own, left_own, wide_edge, left_edge,
+    out, window, wide, left, right, acc, order, codes, blank, order_s, codes_s, todo, sems,
+):
     messages = a_rows.shape[0] // 16
     slots = messages * CAP
+    blocks = own.shape[1] // TB
     row = lax.broadcasted_iota(jnp.int32, (8, TB), 0)
-    fetches = [
-        pltpu.make_async_copy(wide_far, wide, sems.at[3]),
-        pltpu.make_async_copy(left_far, left, sems.at[4]),
-    ]
+    fetches = []
+    for edge, inner, there in ((wide_edge, wide_own, wide), (left_edge, left_own, left)):
+        fetches.append((edge.at[0:MB], there.at[0:MB]))
+        fetches.append((inner, there.at[MB : MB + blocks]))
+        fetches.append((edge.at[MB : 2 * MB], there.at[MB + blocks : 2 * MB + blocks]))
+    fetches.append((below, window.at[:, 0 : MB * TB]))
+    fetches.append((own, window.at[:, MB * TB : (MB + blocks) * TB]))
+    fetches.append((above, window.at[:, (MB + blocks) * TB : (2 * MB + blocks) * TB]))
+    fetches = [pltpu.make_async_copy(a, b, sems.at[3 + i]) for i, (a, b) in enumerate(fetches)]
     for fetch in fetches:
         fetch.start()
     sort_pairs(a_rows, order, codes)
@@ -145,21 +167,18 @@
         copy.start()
     acc[...] = jnp.zeros_like(acc)
 
-    def turn(g, c):
-        right_terms(a_rows, right, g)
-        return c
-
-    lax.fori_loop(0, messages // 8, turn, 0)
     for copy in copies:
         copy.wait()
 
-    def put(m, c):
-        for e in range(16):
-            p = order_s[e, m]
-            todo[p] = codes_s[e, m]
-        return c
-
-    lax.fori_loop(0, messages, put, 0, unroll=2)
+    def arrange(g, c):
+        for i in range(8):
+            m = g * 8 + i
+            for e in range(16):
+                todo[order_s[e, m]] = codes_s[e, m]
+            right_terms(a_rows, right, m)
+        return c
+
+    lax.fori_loop(0, messages // 8, arrange, 0)
     for fetch in fetches:
         fetch.wait()
     groups = order_s[16, 0]
@@ -167,17 +186,12 @@
     def group(code):
         w = code[0] & (TB - 1)
         slot = [jnp.minimum(lax.shift_right_logical(c, 7), slots - 1) for c in code]
-        base = [lax.shift_right_logical(s, 2) * 16 + (s & 3) for s in slot]
         tile = window[:, pl.ds(pl.multiple_of(w * TB, TB), TB)]
 
-        spare = jnp.zeros((32 - TERMS, TB), F32)
-        terms = [
-            jnp.concatenate([right[pl.ds(pl.multiple_of(t * TERMS, 8), TERMS), :], spare], axis=0)
-            for t in slot
-        ]
-        terms = jnp.concatenate(terms, axis=1).astype(BF16)
-        apart = jnp.dot(left[w][:, :32], terms, preferred_element_type=F32)
-        spread = [jnp.broadcast_to(a_rows[pl.ds(b + 8, 1), :], (8, TB)) for b in base]
+        terms = [right[pl.ds(pl.multiple_of(t * TERMS, TERMS), TERMS), :] for t in slot]
+        terms = jnp.concatenate(terms, axis=1)
+        apart = jnp.dot(left[w][:, :TERMS], terms, preferred_element_type=F32)
+        spread = [jnp.broadcast_to(a_rows[pl.ds(4 * t + 2, 1), :], (8, TB)) for t in slot]
         high, low = [[] for _ in code], [[] for _ in code]
         for strip in range(0, TB, 16):
             s = [wide[w, strip + h : strip + h + 8, :] for h in (0, 8)]
@@ -226,24 +240,27 @@
 
 def unpack_kernel(place, back, matched, prob):
     def one(b, c):
-        slot = place[b]
-        base = slot // CAP * 24 + slot % CAP * 6
+        base = place[b]
         lanes = pl.ds(pl.multiple_of(b * TB, TB), TB)
         for q in range(5):
             matched[q : q + 1, lanes] = back[pl.ds(base + q, 1), :]
         prob[pl.ds(b, 1), :] = back[pl.ds(base + 5, 1), :]
         return c
 
-    lax.fori_loop(0, place.shape[0], one, 0, unroll=4)
+    lax.fori_loop(0, place.shape[0], one, 0, unroll=8)
 
 
 VMEM = pl.BlockSpec(memory_space=pltpu.VMEM)
-FAR = pl.BlockSpec(memory_space=pl.ANY)
+FAR = pl.BlockSpec(memory_space=pltpu.HBM)
 SMEM = pl.BlockSpec(memory_space=pltpu.SMEM)
 
 
 def params(mib):
     return pltpu.CompilerParams(vmem_limit_bytes=mib * 2**20)
+
+
+def far(*arrays):
+    return [pltpu.with_memory_space_constraint(x, pltpu.HBM) for x in arrays]
 
 
 def prepare_call(window):
@@ -262,18 +279,20 @@
     )(window)
 
 
-def match_call(a_rows, window, wide, left):
+def match_call(a_rows, own, below, above, *prepared):
     messages = a_rows.shape[0] // 16
+    blocks = own.shape[1] // TB + 2 * MB
     size = -(-list_size(messages) // 1024) * 1024
     return pl.pallas_call(
         match_kernel,
         out_shape=jax.ShapeDtypeStruct((messages, CAP * 6, TB), F32),
-        in_specs=[VMEM, VMEM, FAR, FAR],
+        in_specs=[VMEM] + [FAR] * 7,
         out_specs=VMEM,
         scratch_shapes=[
-            pltpu.VMEM(wide.shape, wide.dtype),
-            pltpu.VMEM(left.shape, left.dtype),
-            pltpu.VMEM((messages * CAP * TERMS, TB), F32),
+            pltpu.VMEM((8, blocks * TB), F32),
+            pltpu.VMEM((blocks, TB, TB), F32),
+            pltpu.VMEM((blocks, TB, TB), BF16),
+            pltpu.VMEM((messages * CAP * TERMS, TB), BF16),
             pltpu.VMEM((messages * CAP + 1, 8, TB), F32),
             pltpu.VMEM((24, messages), jnp.int32),
             pltpu.VMEM((16, messages), jnp.int32),
@@ -281,11 +300,11 @@
             pltpu.SMEM((24, messages), jnp.int32),
             pltpu.SMEM((16, messages), jnp.int32),
             pltpu.SMEM((size,), jnp.int32),
-            pltpu.SemaphoreType.DMA((5,)),
+            pltpu.SemaphoreType.DMA((12,)),
         ],
         compiler_params=params(28),
         name="match",
-    )(a_rows, window, wide, left)
+    )(a_rows, *far(own, below, above, *prepared))
 
 
 def body(a_coord, a_var, dest, cand, cand_count, b_coord, b_var, b_prior, b_flux):
@@ -300,12 +319,17 @@
             jax.ShapeDtypeStruct((devices * 16, TB), F32),
             jax.ShapeDtypeStruct((count,), jnp.int32),
         ),
-        in_specs=[SMEM, VMEM, VMEM, VMEM],
+        in_specs=[SMEM, FAR, FAR, VMEM],
         out_specs=(VMEM, SMEM),
-        scratch_shapes=[pltpu.SMEM((devices,), jnp.int32)],
+        scratch_shapes=[
+            pltpu.SMEM((devices,), jnp.int32),
+            pltpu.VMEM(a_coord.shape, F32),
+            pltpu.VMEM((count, TB), F32),
+            pltpu.SemaphoreType.DMA((2,)),
+        ],
         compiler_params=params(16),
         name="pack",
-    )(dest.reshape(count), a_coord, a_var.reshape(count, TB), labels)
+    )(dest.reshape(count), *far(a_coord, a_var.reshape(count, TB)), labels)
     send, b_coord, b_flux, b_var, b_prior = lax.optimization_barrier(
         (send, b_coord, b_flux, b_var, b_prior)
     )
@@ -315,13 +339,16 @@
     own = jnp.concatenate(
         [b_coord, b_flux, b_var[None, :], b_prior[None, :], jnp.zeros_like(b_var)[None, :]], axis=0
     )
+    inner = prepare_call(own)
     width = MB * TB
+    ends = jnp.concatenate([own[:, -width:], own[:, :width]], axis=1)
+    ends, *inner = lax.optimization_barrier((ends, *inner))
     up = [(i, i + 1) for i in range(zones - 1)]
-    below = lax.ppermute(own[:, -width:], "zone", up)
-    above = lax.ppermute(own[:, :width], "zone", [(j, i) for i, j in up])
-    window = jnp.concatenate([below, own, above], axis=1)
+    below = lax.ppermute(ends[:, :width], "zone", up)
+    above = lax.ppermute(ends[:, width:], "zone", [(j, i) for i, j in up])
+    edge = prepare_call(jnp.concatenate([below, above], axis=1))
     slots = devices * CAP
-    result = match_call(got.reshape(devices * 16, TB), window, *prepare_call(window))
+    result = match_call(got.reshape(devices * 16, TB), own, below, above, *inner, *edge)
     back = lax.all_to_all(result, ("zone", "tile"), split_axis=0, concat_axis=0, tiled=True)
     matched, prob = pl.pallas_call(
         unpack_kernel,

time: 125 us -> 110 us (0.88)
  waiting for transfers between devices: 11.5 us -> 4.56 us
  local copies, waits for them, and re-layouts: 11.8 us -> 6.2 us
  Pallas kernels: 38.3 us -> 34.5 us
  blocking collectives: 44.1 us -> 45.9 us
    all_to_all x1, waiting for transfers between devices: 11.5 us -> 2.77 us  [body(): lax.all_to_all(send.reshape(devices, 16, TB), ('zone', 'tile'), split_axi...]
    unnamed x14 -> x24, local copies, waits for them, and re-layouts: 10.5 us -> 5.76 us
    pallas_call x1, Pallas kernels: 27.5 us -> 24.6 us  [match_call(): pl.pallas_call(match_kernel, out_shape=jax.ShapeDtypeStruct((messages, CA...]
    all_to_all x1, blocking collectives: 44.1 us -> 45.9 us  [body(): lax.all_to_all(result, ('zone', 'tile'), split_axis=0, concat_axis=0, til...]
    ppermute x2, waiting for transfers between devices: 0.01 us -> 1.79 us  [the longest x1 1.79 us: body(): above = lax.ppermute(ends[:, width:], 'zone', [(j, i) for i, j in up])]
    pallas_call x1, Pallas kernels: 3.87 us -> 2.24 us  [body(): pl.pallas_call(unpack_kernel, out_shape=(jax.ShapeDtypeStruct((5, count *...]
    pallas_call x1 -> x2, Pallas kernels: 3.69 us -> 3.69 us  [prepare_call(): pl.pallas_call(prepare_kernel, out_shape=(jax.ShapeDtypeStruct((blocks, T...]
  transfers between devices with their start and end apart: 3 -> 3, of which waited for: 1 -> 2; matrix products, arithmetic and copies ran while one was open for 0% -> 0% of each run, Pallas kernels for 3% -> 3%
where the time goes in v3:
time: 110 us
  blocking collectives  45.9 us (42%)
  Pallas kernels  34.5 us (31%)
  starting transfers between devices  16.8 us (15%)
  local copies, waits for them, and re-layouts  6.2 us (6%)
  waiting for transfers between devices  4.56 us (4%)
    all_to_all x1, blocking collectives, body(): lax.all_to_all(result, ('zone', 'tile'), split_axis=0, concat_axis=0, til...  45.9 us
    pallas_call x1, Pallas kernels, match_call(): pl.pallas_call(match_kernel, out_shape=jax.ShapeDtypeStruct((messages, CA...  24.6 us
    all_to_all x1, starting transfers between devices, body(): lax.all_to_all(send.reshape(devices, 16, TB), ('zone', 'tile'), split_axi...  11.5 us
    unnamed x24, local copies, waits for them, and re-layouts  5.76 us
    ppermute x1, starting transfers between devices, body(): below = lax.ppermute(ends[:, :width], 'zone', up)  4.04 us
    pallas_call x1, Pallas kernels, body(): pl.pallas_call(pack_kernel, out_shape=(jax.ShapeDtypeStruct((devices * 16...  3.97 us
    pallas_call x2, Pallas kernels, prepare_call(): pl.pallas_call(prepare_kernel, out_shape=(jax.ShapeDtypeStruct((blocks, T...  3.69 us
    all_to_all x1, waiting for transfers between devices, body(): lax.all_to_all(send.reshape(devices, 16, TB), ('zone', 'tile'), split_axi...  2.77 us
  transfers between devices with their start and end apart: 3, of which 2 were waited for; matrix products, arithmetic and copies ran while one was open for 0% of the time, Pallas kernels for 3%

profile of v3, /device:TPU:1, one launch (start us, length us, event | category | flops | bytes accessed | tf_op | source)
XLA Modules:
  0.0 109.6 jit_solution(3634977874974534959)
XLA Ops:
  0.6 0.0 copy-start.8
  0.6 0.0 copy-start.11
  0.7 0.0 copy-start.10
  0.7 0.0 copy-start.9
  0.7 0.8 add_convert_fusion
  1.4 0.1 copy.14
  1.6 0.0 copy-start.5
  1.6 0.7 copy-done.5
  2.3 4.0 %pack.1 = (f32[2048,128]{1,0:T(8,128)}, s32[256]{0:T(256)S(1)}) custom-call(s32[256]{0:T(256)S(1)} %bitcast.10, f32[2,32768]{1,0:T(2,128)} %far_coord.1, f32[256,128]{1,0:T(8,128)} %bitcast.11, f32[256,128]{1,0:T(8,128)S(1)} %pad.4.labels), custom_call_target="tpu_custom_call" | custom-call | tf_op jit(solution)/shard_map/pack/pallas_call | solution.py:316
  6.3 11.5 %all-to-all-start = ((f32[128,16,128]{2,1,0:T(8,128)}), f32[128,16,128]{2,1,0:T(8,128)S(1)}, u32[]{:S(2)}, u32[]{:S(2)}) async-start(f32[128,16,128]{2,1,0:T(8,128)} %bitcast.2), calls=%async_computation | async-start | bytes 2097152 | tf_op jit(solution)/shard_map/all_to_all | solution.py:336
  17.8 0.0 copy-done.8
  17.8 0.0 copy-done.11
  17.8 0.0 copy-done.10
  17.8 0.0 copy-done.9
  17.8 0.3 concatenate.13.window.own
  18.1 0.0 copy-start.2
  18.1 3.0 %prepare.2 = (f32[64,128,128]{2,1,0:T(8,128)S(1)}, bf16[64,128,128]{2,1,0:T(8,128)(2,1)S(1)}) custom-call(f32[8,8192]{1,0:T(8,128)S(1)} %concatenate.13.window.own), custom_call_target="tpu_custom_call" | custom-call | flops 100000000 | bytes 10000000 | tf_op jit(solution)/shard_map/prepare/pallas_call | solution.py:268
  21.1 0.0 copy-start
  21.1 1.9 %copy-done = f32[64,128,128]{2,1,0:T(8,128)} copy-done((f32[64,128,128]{2,1,0:T(8,128)}, f32[64,128,128]{2,1,0:T(8,128)S(1)}, u32[]{:S(2)}) %copy-start) | copy-done | bytes 4194328
  23.0 0.0 copy-start.1
  23.0 1.3 %copy-done.1 = bf16[64,128,128]{2,1,0:T(8,128)(2,1)} copy-done((bf16[64,128,128]{2,1,0:T(8,128)(2,1)}, bf16[64,128,128]{2,1,0:T(8,128)(2,1)S(1)}, u32[]{:S(2)}) %copy-start.1) | copy-done | bytes 2097176
  24.4 1.3 %collective-permute-start.1 = (f32[8,1024]{1,0:T(8,128)S(1)}, f32[8,1024]{1,0:T(8,128)S(1)}, u32[]{:S(2)}, u32[]{:S(2)}) collective-permute-start(f32[8,1024]{1,0:T(8,128)S(1)} %get-tuple-element.36), channel_id=1, source_target_pairs={{8,0},{16,8},{24,16},{32,24},{40,32},{48,40},{56,48},{64,56},{72,6... | collective-permute-start | bytes 98312 | tf_op jit(solution)/shard_map/ppermute | solution.py:348
  25.7 4.0 %collective-permute-start = (f32[8,1024]{1,0:T(8,128)S(1)}, f32[8,1024]{1,0:T(8,128)S(1)}, u32[]{:S(2)}, u32[]{:S(2)}) collective-permute-start(f32[8,1024]{1,0:T(8,128)S(1)} %get-tuple-element.37), channel_id=1, source_target_pairs={{0,8},{8,16},{16,24},{24,32},{32,40},{40,48},{48,56},{56,64},{64,7... | collective-permute-start | bytes 98312 | tf_op jit(solution)/shard_map/ppermute | solution.py:347
  29.7 1.8 %collective-permute-done.1.above = f32[8,1024]{1,0:T(8,128)S(1)} collective-permute-done((f32[8,1024]{1,0:T(8,128)S(1)}, f32[8,1024]{1,0:T(8,128)S(1)}, u32[]{:S(2)}, u32[]{:S(2)}) %collective-permute-start.1) | collective-permute-done | bytes 32800 | tf_op jit(solution)/shard_map/ppermute | solution.py:348
  31.5 0.0 copy-start.6
  31.5 0.0 collective-permute-done.below
  31.5 0.0 copy-start.7
  31.6 0.7 prepare.3
  32.3 0.0 copy-start.3
  32.3 1.0 copy-done.3
  33.3 0.0 copy-start.4
  33.3 0.8 copy-done.4
  34.1 2.8 %all-to-all-done = f32[128,16,128]{2,1,0:T(8,128)S(1)} async-done(((f32[128,16,128]{2,1,0:T(8,128)}), f32[128,16,128]{2,1,0:T(8,128)S(1)}, u32[]{:S(2)}, u32[]{:S(2)}) %all-to-all-start) | async-done | bytes 1048608 | tf_op jit(solution)/shard_map/all_to_all | solution.py:336
  36.9 0.0 copy-done.2
  36.9 0.0 copy-done.6
  36.9 0.0 copy-done.7
  36.9 24.6 %match.1 = f32[128,24,128]{2,1,0:T(8,128)S(1)} custom-call(f32[2048,128]{1,0:T(8,128)S(1)} %bitcast.9, f32[8,8192]{1,0:T(8,128)} %copy-done.2, f32[8,1024]{1,0:T(8,128)} %copy-done.7, f32[8,1024]{1,0:T(8,128)} %copy-done.6, f32[64,128,128]{2,1,0:T(8,128)} %copy-done, bf16[64,128,128]{2,1,0:T(8,128)(2,1)} %copy-done.1, f32[16,128,128]{2,1,0:T(8,128)} %copy-done.3, ...), custom_call_target="tpu_custom_call" | custom-call | tf_op jit(solution)/shard_map/match/pallas_call | solution.py:286
  61.4 45.9 %all_to_all.10 = f32[128,24,128]{2,1,0:T(8,128)S(1)} all-to-all(f32[128,24,128]{2,1,0:T(8,128)S(1)} %match.1), channel_id=1, replica_groups=mesh['zone'=16,'tile'=8] {'zone','tile'}, dimensions={0} | all-to-all | bytes 3145728 | tf_op jit(solution)/shard_map/all_to_all | solution.py:352
  107.4 2.2 %unpack.1 = (f32[5,32768]{1,0:T(8,128)}, f32[256,128]{1,0:T(8,128)}) custom-call(s32[256]{0:T(256)S(1)} %get-tuple-element.18.place, f32[3072,128]{1,0:T(8,128)S(1)} %bitcast.8), custom_call_target="tpu_custom_call" | custom-call | tf_op jit(solution)/shard_map/unpack/pallas_call | solution.py:353
  (6 shorter events, 0.1 us)
Async XLA Ops:
  0.6 17.2 %copy-start.8 = (f32[3,8192]{1,0:T(4,128)S(1)}, f32[3,8192]{1,0:T(4,128)}, u32[]{:S(2)}) copy-start(f32[3,8192]{1,0:T(4,128)} %param.17) | copy-start | bytes 294916
  0.6 17.2 %copy-start.11 = (f32[8192]{0:T(1024)S(1)}, f32[8192]{0:T(1024)}, u32[]{:S(2)}) copy-start(f32[8192]{0:T(1024)} %param.16) | copy-start | bytes 98308
  0.7 17.2 %copy-start.10 = (f32[8192]{0:T(1024)S(1)}, f32[8192]{0:T(1024)}, u32[]{:S(2)}) copy-start(f32[8192]{0:T(1024)} %param.15) | copy-start | bytes 98308
  0.7 17.2 %copy-start.9 = (f32[2,8192]{1,0:T(2,128)S(1)}, f32[2,8192]{1,0:T(2,128)}, u32[]{:S(2)}) copy-start(f32[2,8192]{1,0:T(2,128)} %param.14) | copy-start | bytes 196612
  1.6 0.7 copy-start.5
  6.3 30.6 %all-to-all-start = ((f32[128,16,128]{2,1,0:T(8,128)}), f32[128,16,128]{2,1,0:T(8,128)S(1)}, u32[]{:S(2)}, u32[]{:S(2)}) async-start(f32[128,16,128]{2,1,0:T(8,128)} %bitcast.2), calls=%async_computation | async-start | bytes 2097152 | tf_op jit(solution)/shard_map/all_to_all | solution.py:336
  18.1 18.7 %copy-start.2 = (f32[8,8192]{1,0:T(8,128)}, f32[8,8192]{1,0:T(8,128)S(1)}, u32[]{:S(2)}) copy-start(f32[8,8192]{1,0:T(8,128)S(1)} %concatenate.13.window.own) | copy-start | bytes 786436
  21.1 1.9 %copy-start = (f32[64,128,128]{2,1,0:T(8,128)}, f32[64,128,128]{2,1,0:T(8,128)S(1)}, u32[]{:S(2)}) copy-start(f32[64,128,128]{2,1,0:T(8,128)S(1)} %get-tuple-element.28.wide_own) | copy-start | bytes 12582916
  23.0 1.3 %copy-start.1 = (bf16[64,128,128]{2,1,0:T(8,128)(2,1)}, bf16[64,128,128]{2,1,0:T(8,128)(2,1)S(1)}, u32[]{:S(2)}) copy-start(bf16[64,128,128]{2,1,0:T(8,128)(2,1)S(1)} %get-tuple-element.29.left_own) | copy-start | bytes 6291460
  24.4 7.1 %collective-permute-start.1 = (f32[8,1024]{1,0:T(8,128)S(1)}, f32[8,1024]{1,0:T(8,128)S(1)}, u32[]{:S(2)}, u32[]{:S(2)}) collective-permute-start(f32[8,1024]{1,0:T(8,128)S(1)} %get-tuple-element.36), channel_id=1, source_target_pairs={{8,0},{16,8},{24,16},{32,24},{40,32},{48,40},{56,48},{64,56},{72,6... | collective-permute-start | bytes 98312 | tf_op jit(solution)/shard_map/ppermute | solution.py:348
  25.7 5.8 %collective-permute-start = (f32[8,1024]{1,0:T(8,128)S(1)}, f32[8,1024]{1,0:T(8,128)S(1)}, u32[]{:S(2)}, u32[]{:S(2)}) collective-permute-start(f32[8,1024]{1,0:T(8,128)S(1)} %get-tuple-element.37), channel_id=1, source_target_pairs={{0,8},{8,16},{16,24},{24,32},{32,40},{40,48},{48,56},{56,64},{64,7... | collective-permute-start | bytes 98312 | tf_op jit(solution)/shard_map/ppermute | solution.py:347
  31.5 5.3 %copy-start.6 = (f32[8,1024]{1,0:T(8,128)}, f32[8,1024]{1,0:T(8,128)S(1)}, u32[]{:S(2)}) copy-start(f32[8,1024]{1,0:T(8,128)S(1)} %collective-permute-done.1.above) | copy-start | bytes 98308
  31.5 5.3 %copy-start.7 = (f32[8,1024]{1,0:T(8,128)}, f32[8,1024]{1,0:T(8,128)S(1)}, u32[]{:S(2)}) copy-start(f32[8,1024]{1,0:T(8,128)S(1)} %collective-permute-done.below) | copy-start | bytes 98308
  32.3 1.0 copy-start.3
  33.3 0.8 copy-start.4

commit v4 on v3

--- a/solution.py
+++ b/solution.py
@@ -12,10 +12,11 @@
 K = 4
 MB = 8
 CAP = 4
-UNROLL = 20
+UNROLL = 32
 GROUP = 2
 TERMS = 32
 DEAD = 127
+SHIFT = 17
 SCALE = math.sqrt(0.5 / math.log(2.0))
 F32 = jnp.float32
 BF16 = jnp.bfloat16
@@ -88,7 +89,7 @@
             right[pl.ds(pl.multiple_of(start, TERMS), TERMS), :] = parts.astype(BF16)
 
 
-def sort_pairs(a_rows, order, codes):
+def sort_pairs(a_rows, order):
     messages = a_rows.shape[0] // 16
     line = lax.broadcasted_iota(jnp.int32, (TB, messages), 0).astype(F32)
     lane = lax.broadcasted_iota(jnp.int32, (1, messages), 1)
@@ -112,8 +113,9 @@
     for row in range(16):
         spot = jnp.sum(marks[row] * place, axis=0, keepdims=True)
         live = keys[row] < DEAD
-        order[row : row + 1, :] = jnp.where(live, spot, float(order_dump(messages))).astype(jnp.int32)
-        codes[row : row + 1, :] = (lane * CAP + row % 4) * TB + keys[row].astype(jnp.int32)
+        spot = jnp.where(live, spot, float(order_dump(messages))).astype(jnp.int32)
+        code = (lane * CAP + row % 4) * TB + keys[row].astype(jnp.int32)
+        order[row : row + 1, :] = spot * (1 << SHIFT) + code
         if row < 15:
             place = place + marks[row]
     order[16:17, :] = first[DEAD : DEAD + 1].astype(jnp.int32)
@@ -139,7 +141,7 @@
 
 def match_kernel(
     a_rows, own, below, above, wide_own, left_own, wide_edge, left_edge,
-    out, window, wide, left, right, acc, order, codes, blank, order_s, codes_s, todo, sems,
+    out, window, wide, left, right, acc, order, blank, order_s, todo, sems,
 ):
     messages = a_rows.shape[0] // 16
     slots = messages * CAP
@@ -153,15 +155,14 @@
     fetches.append((below, window.at[:, 0 : MB * TB]))
     fetches.append((own, window.at[:, MB * TB : (MB + blocks) * TB]))
     fetches.append((above, window.at[:, (MB + blocks) * TB : (2 * MB + blocks) * TB]))
-    fetches = [pltpu.make_async_copy(a, b, sems.at[3 + i]) for i, (a, b) in enumerate(fetches)]
+    fetches = [pltpu.make_async_copy(a, b, sems.at[2 + i]) for i, (a, b) in enumerate(fetches)]
     for fetch in fetches:
         fetch.start()
-    sort_pairs(a_rows, order, codes)
+    sort_pairs(a_rows, order)
     blank[...] = jnp.full(blank.shape, slots * TB, jnp.int32)
     copies = [
         pltpu.make_async_copy(order, order_s, sems.at[0]),
-        pltpu.make_async_copy(codes, codes_s, sems.at[1]),
-        pltpu.make_async_copy(blank, todo, sems.at[2]),
+        pltpu.make_async_copy(blank, todo, sems.at[1]),
     ]
     for copy in copies:
         copy.start()
@@ -171,14 +172,14 @@
         copy.wait()
 
     def arrange(g, c):
-        for i in range(8):
-            m = g * 8 + i
-            for e in range(16):
-                todo[order_s[e, m]] = codes_s[e, m]
-            right_terms(a_rows, right, m)
-        return c
-
-    lax.fori_loop(0, messages // 8, arrange, 0)
+        for m in range(messages):
+            word = order_s[g, m]
+            todo[lax.shift_right_logical(word, SHIFT)] = word
+        for m in range(messages // 16):
+            right_terms(a_rows, right, g * (messages // 16) + m)
+        return c
+
+    lax.fori_loop(0, 16, arrange, 0)
     for fetch in fetches:
         fetch.wait()
     groups = order_s[16, 0]
@@ -217,7 +218,7 @@
     def chunk(c, carry):
         done = []
         for k in range(UNROLL):
-            code = [todo[(c * UNROLL + k) * GROUP + e] for e in range(GROUP)]
+            code = [todo[(c * UNROLL + k) * GROUP + e] & ((1 << SHIFT) - 1) for e in range(GROUP)]
             done.append((code, group(code)))
         for code, total in done:
             for e in range(GROUP):
@@ -295,12 +296,10 @@
             pltpu.VMEM((messages * CAP * TERMS, TB), BF16),
             pltpu.VMEM((messages * CAP + 1, 8, TB), F32),
             pltpu.VMEM((24, messages), jnp.int32),
-            pltpu.VMEM((16, messages), jnp.int32),
             pltpu.VMEM((size,), jnp.int32),
             pltpu.SMEM((24, messages), jnp.int32),
-            pltpu.SMEM((16, messages), jnp.int32),
             pltpu.SMEM((size,), jnp.int32),
-            pltpu.SemaphoreType.DMA((12,)),
+            pltpu.SemaphoreType.DMA((11,)),
         ],
         compiler_params=params(28),
         name="match",

time: 110 us -> 107 us (0.973)
  blocking collectives: 45.9 us -> 44.2 us
  Pallas kernels: 34.5 us -> 33.4 us
    all_to_all x1, blocking collectives: 45.9 us -> 44.2 us  [body(): lax.all_to_all(result, ('zone', 'tile'), split_axis=0, concat_axis=0, til...]
where the time goes in v4:
time: 107 us
  blocking collectives  44.2 us (41%)
  Pallas kernels  33.4 us (31%)
  starting transfers between devices  16.8 us (16%)
  local copies, waits for them, and re-layouts  6.2 us (6%)
  waiting for transfers between devices  4.56 us (4%)
    all_to_all x1, blocking collectives, body(): lax.all_to_all(result, ('zone', 'tile'), split_axis=0, concat_axis=0, til...  44.2 us
    pallas_call x1, Pallas kernels, match_call(): pl.pallas_call(match_kernel, out_shape=jax.ShapeDtypeStruct((messages, CA...  23.5 us
    all_to_all x1, starting transfers between devices, body(): lax.all_to_all(send.reshape(devices, 16, TB), ('zone', 'tile'), split_axi...  11.5 us
    unnamed x24, local copies, waits for them, and re-layouts  5.76 us
    ppermute x1, starting transfers between devices, body(): below = lax.ppermute(ends[:, :width], 'zone', up)  4.04 us
    pallas_call x1, Pallas kernels, body(): pl.pallas_call(pack_kernel, out_shape=(jax.ShapeDtypeStruct((devices * 16...  3.97 us
    pallas_call x2, Pallas kernels, prepare_call(): pl.pallas_call(prepare_kernel, out_shape=(jax.ShapeDtypeStruct((blocks, T...  3.69 us
    all_to_all x1, waiting for transfers between devices, body(): lax.all_to_all(send.reshape(devices, 16, TB), ('zone', 'tile'), split_axi...  2.77 us
  transfers between devices with their start and end apart: 3, of which 2 were waited for; matrix products, arithmetic and copies ran while one was open for 0% of the time, Pallas kernels for 3%

profile of v4, /device:TPU:1, one launch (start us, length us, event | category | flops | bytes accessed | tf_op | source)
XLA Modules:
  0.0 106.8 jit_solution(10662135656521872967)
XLA Ops:
  0.6 0.0 copy-start.8
  0.6 0.0 copy-start.11
  0.7 0.0 copy-start.10
  0.7 0.0 copy-start.9
  0.7 0.8 add_convert_fusion
  1.4 0.1 copy.14
  1.6 0.0 copy-start.5
  1.6 0.7 copy-done.5
  2.3 4.0 %pack.1 = (f32[2048,128]{1,0:T(8,128)}, s32[256]{0:T(256)S(1)}) custom-call(s32[256]{0:T(256)S(1)} %bitcast.10, f32[2,32768]{1,0:T(2,128)} %far_coord.1, f32[256,128]{1,0:T(8,128)} %bitcast.11, f32[256,128]{1,0:T(8,128)S(1)} %pad.4.labels), custom_call_target="tpu_custom_call" | custom-call | tf_op jit(solution)/shard_map/pack/pallas_call | solution.py:315
  6.3 11.5 %all-to-all-start = ((f32[128,16,128]{2,1,0:T(8,128)}), f32[128,16,128]{2,1,0:T(8,128)S(1)}, u32[]{:S(2)}, u32[]{:S(2)}) async-start(f32[128,16,128]{2,1,0:T(8,128)} %bitcast.2), calls=%async_computation | async-start | bytes 2097152 | tf_op jit(solution)/shard_map/all_to_all | solution.py:335
  17.8 0.0 copy-done.8
  17.8 0.0 copy-done.11
  17.8 0.0 copy-done.10
  17.8 0.0 copy-done.9
  17.8 0.3 concatenate.13.window.own
  18.1 0.0 copy-start.2
  18.1 3.0 %prepare.2 = (f32[64,128,128]{2,1,0:T(8,128)S(1)}, bf16[64,128,128]{2,1,0:T(8,128)(2,1)S(1)}) custom-call(f32[8,8192]{1,0:T(8,128)S(1)} %concatenate.13.window.own), custom_call_target="tpu_custom_call" | custom-call | flops 100000000 | bytes 10000000 | tf_op jit(solution)/shard_map/prepare/pallas_call | solution.py:269
  21.1 0.0 copy-start
  21.1 1.9 %copy-done = f32[64,128,128]{2,1,0:T(8,128)} copy-done((f32[64,128,128]{2,1,0:T(8,128)}, f32[64,128,128]{2,1,0:T(8,128)S(1)}, u32[]{:S(2)}) %copy-start) | copy-done | bytes 4194328
  23.0 0.0 copy-start.1
  23.0 1.3 %copy-done.1 = bf16[64,128,128]{2,1,0:T(8,128)(2,1)} copy-done((bf16[64,128,128]{2,1,0:T(8,128)(2,1)}, bf16[64,128,128]{2,1,0:T(8,128)(2,1)S(1)}, u32[]{:S(2)}) %copy-start.1) | copy-done | bytes 2097176
  24.4 1.3 %collective-permute-start.1 = (f32[8,1024]{1,0:T(8,128)S(1)}, f32[8,1024]{1,0:T(8,128)S(1)}, u32[]{:S(2)}, u32[]{:S(2)}) collective-permute-start(f32[8,1024]{1,0:T(8,128)S(1)} %get-tuple-element.36), channel_id=1, source_target_pairs={{8,0},{16,8},{24,16},{32,24},{40,32},{48,40},{56,48},{64,56},{72,6... | collective-permute-start | bytes 98312 | tf_op jit(solution)/shard_map/ppermute | solution.py:347
  25.7 4.0 %collective-permute-start = (f32[8,1024]{1,0:T(8,128)S(1)}, f32[8,1024]{1,0:T(8,128)S(1)}, u32[]{:S(2)}, u32[]{:S(2)}) collective-permute-start(f32[8,1024]{1,0:T(8,128)S(1)} %get-tuple-element.37), channel_id=1, source_target_pairs={{0,8},{8,16},{16,24},{24,32},{32,40},{40,48},{48,56},{56,64},{64,7... | collective-permute-start | bytes 98312 | tf_op jit(solution)/shard_map/ppermute | solution.py:346
  29.7 1.8 %collective-permute-done.1.above = f32[8,1024]{1,0:T(8,128)S(1)} collective-permute-done((f32[8,1024]{1,0:T(8,128)S(1)}, f32[8,1024]{1,0:T(8,128)S(1)}, u32[]{:S(2)}, u32[]{:S(2)}) %collective-permute-start.1) | collective-permute-done | bytes 32800 | tf_op jit(solution)/shard_map/ppermute | solution.py:347
  31.5 0.0 copy-start.6
  31.5 0.0 collective-permute-done.below
  31.5 0.0 copy-start.7
  31.6 0.7 prepare.3
  32.3 0.0 copy-start.3
  32.3 1.0 copy-done.3
  33.3 0.0 copy-start.4
  33.3 0.8 copy-done.4
  34.1 2.8 %all-to-all-done = f32[128,16,128]{2,1,0:T(8,128)S(1)} async-done(((f32[128,16,128]{2,1,0:T(8,128)}), f32[128,16,128]{2,1,0:T(8,128)S(1)}, u32[]{:S(2)}, u32[]{:S(2)}) %all-to-all-start) | async-done | bytes 1048608 | tf_op jit(solution)/shard_map/all_to_all | solution.py:335
  36.9 0.0 copy-done.2
  36.9 0.0 copy-done.6
  36.9 0.0 copy-done.7
  36.9 23.5 %match.1 = f32[128,24,128]{2,1,0:T(8,128)S(1)} custom-call(f32[2048,128]{1,0:T(8,128)S(1)} %bitcast.9, f32[8,8192]{1,0:T(8,128)} %copy-done.2, f32[8,1024]{1,0:T(8,128)} %copy-done.7, f32[8,1024]{1,0:T(8,128)} %copy-done.6, f32[64,128,128]{2,1,0:T(8,128)} %copy-done, bf16[64,128,128]{2,1,0:T(8,128)(2,1)} %copy-done.1, f32[16,128,128]{2,1,0:T(8,128)} %copy-done.3, ...), custom_call_target="tpu_custom_call" | custom-call | tf_op jit(solution)/shard_map/match/pallas_call | solution.py:287
  60.3 44.2 %all_to_all.10 = f32[128,24,128]{2,1,0:T(8,128)S(1)} all-to-all(f32[128,24,128]{2,1,0:T(8,128)S(1)} %match.1), channel_id=1, replica_groups=mesh['zone'=16,'tile'=8] {'zone','tile'}, dimensions={0} | all-to-all | bytes 3145728 | tf_op jit(solution)/shard_map/all_to_all | solution.py:351
  104.6 2.2 %unpack.1 = (f32[5,32768]{1,0:T(8,128)}, f32[256,128]{1,0:T(8,128)}) custom-call(s32[256]{0:T(256)S(1)} %get-tuple-element.18.place, f32[3072,128]{1,0:T(8,128)S(1)} %bitcast.8), custom_call_target="tpu_custom_call" | custom-call | tf_op jit(solution)/shard_map/unpack/pallas_call | solution.py:352
  (6 shorter events, 0.1 us)
Async XLA Ops:
  0.6 17.2 %copy-start.8 = (f32[3,8192]{1,0:T(4,128)S(1)}, f32[3,8192]{1,0:T(4,128)}, u32[]{:S(2)}) copy-start(f32[3,8192]{1,0:T(4,128)} %param.17) | copy-start | bytes 294916
  0.6 17.2 %copy-start.11 = (f32[8192]{0:T(1024)S(1)}, f32[8192]{0:T(1024)}, u32[]{:S(2)}) copy-start(f32[8192]{0:T(1024)} %param.16) | copy-start | bytes 98308
  0.7 17.2 %copy-start.10 = (f32[8192]{0:T(1024)S(1)}, f32[8192]{0:T(1024)}, u32[]{:S(2)}) copy-start(f32[8192]{0:T(1024)} %param.15) | copy-start | bytes 98308
  0.7 17.2 %copy-start.9 = (f32[2,8192]{1,0:T(2,128)S(1)}, f32[2,8192]{1,0:T(2,128)}, u32[]{:S(2)}) copy-start(f32[2,8192]{1,0:T(2,128)} %param.14) | copy-start | bytes 196612
  1.6 0.7 copy-start.5
  6.3 30.6 %all-to-all-start = ((f32[128,16,128]{2,1,0:T(8,128)}), f32[128,16,128]{2,1,0:T(8,128)S(1)}, u32[]{:S(2)}, u32[]{:S(2)}) async-start(f32[128,16,128]{2,1,0:T(8,128)} %bitcast.2), calls=%async_computation | async-start | bytes 2097152 | tf_op jit(solution)/shard_map/all_to_all | solution.py:335
  18.1 18.7 %copy-start.2 = (f32[8,8192]{1,0:T(8,128)}, f32[8,8192]{1,0:T(8,128)S(1)}, u32[]{:S(2)}) copy-start(f32[8,8192]{1,0:T(8,128)S(1)} %concatenate.13.window.own) | copy-start | bytes 786436
  21.1 1.9 %copy-start = (f32[64,128,128]{2,1,0:T(8,128)}, f32[64,128,128]{2,1,0:T(8,128)S(1)}, u32[]{:S(2)}) copy-start(f32[64,128,128]{2,1,0:T(8,128)S(1)} %get-tuple-element.28.wide_own) | copy-start | bytes 12582916
  23.0 1.3 %copy-start.1 = (bf16[64,128,128]{2,1,0:T(8,128)(2,1)}, bf16[64,128,128]{2,1,0:T(8,128)(2,1)S(1)}, u32[]{:S(2)}) copy-start(bf16[64,128,128]{2,1,0:T(8,128)(2,1)S(1)} %get-tuple-element.29.left_own) | copy-start | bytes 6291460
  24.4 7.1 %collective-permute-start.1 = (f32[8,1024]{1,0:T(8,128)S(1)}, f32[8,1024]{1,0:T(8,128)S(1)}, u32[]{:S(2)}, u32[]{:S(2)}) collective-permute-start(f32[8,1024]{1,0:T(8,128)S(1)} %get-tuple-element.36), channel_id=1, source_target_pairs={{8,0},{16,8},{24,16},{32,24},{40,32},{48,40},{56,48},{64,56},{72,6... | collective-permute-start | bytes 98312 | tf_op jit(solution)/shard_map/ppermute | solution.py:347
  25.7 5.8 %collective-permute-start = (f32[8,1024]{1,0:T(8,128)S(1)}, f32[8,1024]{1,0:T(8,128)S(1)}, u32[]{:S(2)}, u32[]{:S(2)}) collective-permute-start(f32[8,1024]{1,0:T(8,128)S(1)} %get-tuple-element.37), channel_id=1, source_target_pairs={{0,8},{8,16},{16,24},{24,32},{32,40},{40,48},{48,56},{56,64},{64,7... | collective-permute-start | bytes 98312 | tf_op jit(solution)/shard_map/ppermute | solution.py:346
  31.5 5.3 %copy-start.6 = (f32[8,1024]{1,0:T(8,128)}, f32[8,1024]{1,0:T(8,128)S(1)}, u32[]{:S(2)}) copy-start(f32[8,1024]{1,0:T(8,128)S(1)} %collective-permute-done.1.above) | copy-start | bytes 98308
  31.5 5.3 %copy-start.7 = (f32[8,1024]{1,0:T(8,128)}, f32[8,1024]{1,0:T(8,128)S(1)}, u32[]{:S(2)}) copy-start(f32[8,1024]{1,0:T(8,128)S(1)} %collective-permute-done.below) | copy-start | bytes 98308
  32.3 1.0 copy-start.3
  33.3 0.8 copy-start.4

commit v5 on v4

--- a/solution.py
+++ b/solution.py
@@ -129,14 +129,33 @@
     return order_dump(messages) + 1
 
 
-def prepare_kernel(window, wide, left):
-    def one(w, c):
-        tile = window[:, pl.ds(pl.multiple_of(w * TB, TB), TB)]
-        wide[w] = jnp.broadcast_to(-tile[5:6], (TB, TB)).T
-        left[w] = left_terms(tile).T.astype(BF16)
-        return c
-
-    lax.fori_loop(0, wide.shape[0], one, 0, unroll=4)
+def prepare_kernel(window, far_wide, far_left, wide, left, sems):
+    runs = wide.shape[0] // 4
+
+    def copies(run):
+        part = pl.ds(run * 4, 4)
+        return [
+            pltpu.make_async_copy(near.at[part], there.at[part], sems.at[i, run])
+            for i, (near, there) in enumerate(((wide, far_wide), (left, far_left)))
+        ]
+
+    def make(run, c):
+        for k in range(4):
+            w = run * 4 + k
+            tile = window[:, pl.ds(pl.multiple_of(w * TB, TB), TB)]
+            wide[w] = jnp.broadcast_to(-tile[5:6], (TB, TB)).T
+            left[w] = left_terms(tile).T.astype(BF16)
+        for copy in copies(run):
+            copy.start()
+        return c
+
+    def end(run, c):
+        for copy in copies(run):
+            copy.wait()
+        return c
+
+    lax.fori_loop(0, runs, make, 0)
+    lax.fori_loop(0, runs, end, 0)
 
 
 def match_kernel(
@@ -268,12 +287,14 @@
     blocks = window.shape[1] // TB
     return pl.pallas_call(
         prepare_kernel,
-        out_shape=(
-            jax.ShapeDtypeStruct((blocks, TB, TB), F32),
-            jax.ShapeDtypeStruct((blocks, TB, TB), BF16),
-        ),
+        out_shape=(pltpu.HBM((blocks, TB, TB), F32), pltpu.HBM((blocks, TB, TB), BF16)),
         in_specs=[VMEM],
-        out_specs=(VMEM, VMEM),
+        out_specs=(FAR, FAR),
+        scratch_shapes=[
+            pltpu.VMEM((blocks, TB, TB), F32),
+            pltpu.VMEM((blocks, TB, TB), BF16),
+            pltpu.SemaphoreType.DMA((2, blocks // 4)),
+        ],
         compiler_params=params(16),
         cost_estimate=pl.CostEstimate(flops=10**8, bytes_accessed=10**7, transcendentals=0),
         name="prepare",

time: 107 us -> 104 us (0.972)
  blocking collectives: 44.2 us -> 36.7 us
  Pallas kernels: 33.4 us -> 39.4 us
  local copies, waits for them, and re-layouts: 6.2 us -> 1.14 us
  waiting for transfers between devices: 4.56 us -> 7.78 us
    all_to_all x1, blocking collectives: 44.2 us -> 36.7 us  [body(): lax.all_to_all(result, ('zone', 'tile'), split_axis=0, concat_axis=0, til...]
    unnamed x24 -> x16, local copies, waits for them, and re-layouts: 5.76 us -> 0.7 us
    pallas_call x1, Pallas kernels: 23.5 us -> 27.7 us  [match_call(): pl.pallas_call(match_kernel, out_shape=jax.ShapeDtypeStruct((messages, CA...]
    ppermute x1, waiting for transfers between devices: 1.79 us -> 4.03 us  [body(): above = lax.ppermute(ends[:, width:], 'zone', [(j, i) for i, j in up])]
    pallas_call x2, Pallas kernels: 3.69 us -> 5.53 us  [prepare_call(): pl.pallas_call(prepare_kernel, out_shape=(pltpu.HBM((blocks, TB, TB), F32...]
  transfers between devices with their start and end apart: 3 -> 3, of which waited for: 2 -> 2; matrix products, arithmetic and copies ran while one was open for 0% -> 0% of each run, Pallas kernels for 3% -> 5%
where the time goes in v5:
time: 104 us; the launch traced here: 103 us
  Pallas kernels  39.4 us (38%)
  blocking collectives  36.7 us (35%)
  starting transfers between devices  16.8 us (16%)
  waiting for transfers between devices  7.78 us (7%)
  local copies, waits for them, and re-layouts  1.14 us (1%)
    all_to_all x1, blocking collectives, body(): lax.all_to_all(result, ('zone', 'tile'), split_axis=0, concat_axis=0, til...  36.7 us
    pallas_call x1, Pallas kernels, match_call(): pl.pallas_call(match_kernel, out_shape=jax.ShapeDtypeStruct((messages, CA...  27.7 us
    all_to_all x1, starting transfers between devices, body(): lax.all_to_all(send.reshape(devices, 16, TB), ('zone', 'tile'), split_axi...  11.5 us
    pallas_call x2, Pallas kernels, prepare_call(): pl.pallas_call(prepare_kernel, out_shape=(pltpu.HBM((blocks, TB, TB), F32...  5.53 us
    ppermute x1, starting transfers between devices, body(): below = lax.ppermute(ends[:, :width], 'zone', up)  4.04 us
    ppermute x1, waiting for transfers between devices, body(): above = lax.ppermute(ends[:, width:], 'zone', [(j, i) for i, j in up])  4.03 us
    pallas_call x1, Pallas kernels, body(): pl.pallas_call(pack_kernel, out_shape=(jax.ShapeDtypeStruct((devices * 16...  3.97 us
    all_to_all x1, waiting for transfers between devices, body(): lax.all_to_all(send.reshape(devices, 16, TB), ('zone', 'tile'), split_axi...  3.75 us
  transfers between devices with their start and end apart: 3, of which 2 were waited for; matrix products, arithmetic and copies ran while one was open for 0% of the time, Pallas kernels for 5%

profile of v5, /device:TPU:1, one launch (start us, length us, event | category | flops | bytes accessed | tf_op | source)
XLA Modules:
  0.0 103.5 jit_solution(10374122869510037503)
XLA Ops:
  0.6 0.0 copy-start.4
  0.6 0.0 copy-start.7
  0.7 0.0 copy-start.6
  0.7 0.0 copy-start.5
  0.7 0.8 add_convert_fusion
  1.4 0.1 copy.14
  1.6 0.0 copy-start.1
  1.6 0.7 copy-done.1
  2.3 4.0 %pack.1 = (f32[2048,128]{1,0:T(8,128)}, s32[256]{0:T(256)S(1)}) custom-call(s32[256]{0:T(256)S(1)} %bitcast.10, f32[2,32768]{1,0:T(2,128)} %far_coord.1, f32[256,128]{1,0:T(8,128)} %bitcast.11, f32[256,128]{1,0:T(8,128)S(1)} %pad.4.labels), custom_call_target="tpu_custom_call" | custom-call | tf_op jit(solution)/shard_map/pack/pallas_call | solution.py:336
  6.3 11.5 %all-to-all-start = ((f32[128,16,128]{2,1,0:T(8,128)}), f32[128,16,128]{2,1,0:T(8,128)S(1)}, u32[]{:S(2)}, u32[]{:S(2)}) async-start(f32[128,16,128]{2,1,0:T(8,128)} %bitcast.2), calls=%async_computation | async-start | bytes 2097152 | tf_op jit(solution)/shard_map/all_to_all | solution.py:356
  17.8 0.0 copy-done.4
  17.8 0.0 copy-done.7
  17.8 0.0 copy-done.6
  17.8 0.0 copy-done.5
  17.8 0.3 concatenate.13.window.own
  18.1 0.0 copy-start
  18.1 4.0 %prepare.2 = (f32[64,128,128]{2,1,0:T(8,128)}, bf16[64,128,128]{2,1,0:T(8,128)(2,1)}) custom-call(f32[8,8192]{1,0:T(8,128)S(1)} %concatenate.13.window.own), custom_call_target="tpu_custom_call" | custom-call | flops 100000000 | bytes 10000000 | tf_op jit(solution)/shard_map/prepare/pallas_call | solution.py:288
  22.2 1.3 %collective-permute-start.1 = (f32[8,1024]{1,0:T(8,128)S(1)}, f32[8,1024]{1,0:T(8,128)S(1)}, u32[]{:S(2)}, u32[]{:S(2)}) collective-permute-start(f32[8,1024]{1,0:T(8,128)S(1)} %get-tuple-element.36), channel_id=1, source_target_pairs={{8,0},{16,8},{24,16},{32,24},{40,32},{48,40},{56,48},{64,56},{72,6... | collective-permute-start | bytes 98312 | tf_op jit(solution)/shard_map/ppermute | solution.py:368
  23.5 4.0 %collective-permute-start = (f32[8,1024]{1,0:T(8,128)S(1)}, f32[8,1024]{1,0:T(8,128)S(1)}, u32[]{:S(2)}, u32[]{:S(2)}) collective-permute-start(f32[8,1024]{1,0:T(8,128)S(1)} %get-tuple-element.37), channel_id=1, source_target_pairs={{0,8},{8,16},{16,24},{24,32},{32,40},{40,48},{48,56},{56,64},{64,7... | collective-permute-start | bytes 98312 | tf_op jit(solution)/shard_map/ppermute | solution.py:367
  27.5 4.0 %collective-permute-done.1.above = f32[8,1024]{1,0:T(8,128)S(1)} collective-permute-done((f32[8,1024]{1,0:T(8,128)S(1)}, f32[8,1024]{1,0:T(8,128)S(1)}, u32[]{:S(2)}, u32[]{:S(2)}) %collective-permute-start.1) | collective-permute-done | bytes 32800 | tf_op jit(solution)/shard_map/ppermute | solution.py:368
  31.5 0.0 copy-start.2
  31.5 0.0 collective-permute-done.below
  31.5 0.0 copy-start.3
  31.6 1.5 %prepare.3 = (f32[16,128,128]{2,1,0:T(8,128)}, bf16[16,128,128]{2,1,0:T(8,128)(2,1)}) custom-call(f32[8,2048]{1,0:T(8,128)S(1)} %pad_maximum_fusion.1.window), custom_call_target="tpu_custom_call" | custom-call | flops 100000000 | bytes 10000000 | tf_op jit(solution)/shard_map/prepare/pallas_call | solution.py:288
  33.1 3.7 %all-to-all-done = f32[128,16,128]{2,1,0:T(8,128)S(1)} async-done(((f32[128,16,128]{2,1,0:T(8,128)}), f32[128,16,128]{2,1,0:T(8,128)S(1)}, u32[]{:S(2)}, u32[]{:S(2)}) %all-to-all-start) | async-done | bytes 1048608 | tf_op jit(solution)/shard_map/all_to_all | solution.py:356
  36.9 0.0 copy-done
  36.9 0.0 copy-done.2
  36.9 0.0 copy-done.3
  36.9 27.7 %match.1 = f32[128,24,128]{2,1,0:T(8,128)S(1)} custom-call(f32[2048,128]{1,0:T(8,128)S(1)} %bitcast.9, f32[8,8192]{1,0:T(8,128)} %copy-done, f32[8,1024]{1,0:T(8,128)} %copy-done.3, f32[8,1024]{1,0:T(8,128)} %copy-done.2, f32[64,128,128]{2,1,0:T(8,128)} %get-tuple-element.28.wide_own, bf16[64,128,128]{2,1,0:T(8,128)(2,1)} %get-tuple-element.29.left_own, ...), custom_call_target="tpu_custom_call" | custom-call | tf_op jit(solution)/shard_map/match/pallas_call | solution.py:308
  64.6 36.7 %all_to_all.10 = f32[128,24,128]{2,1,0:T(8,128)S(1)} all-to-all(f32[128,24,128]{2,1,0:T(8,128)S(1)} %match.1), channel_id=1, replica_groups=mesh['zone'=16,'tile'=8] {'zone','tile'}, dimensions={0} | all-to-all | bytes 3145728 | tf_op jit(solution)/shard_map/all_to_all | solution.py:372
  101.2 2.2 %unpack.1 = (f32[5,32768]{1,0:T(8,128)}, f32[256,128]{1,0:T(8,128)}) custom-call(s32[256]{0:T(256)S(1)} %get-tuple-element.18.place, f32[3072,128]{1,0:T(8,128)S(1)} %bitcast.8), custom_call_target="tpu_custom_call" | custom-call | tf_op jit(solution)/shard_map/unpack/pallas_call | solution.py:373
  (6 shorter events, 0.1 us)
Async XLA Ops:
  0.6 17.2 %copy-start.4 = (f32[3,8192]{1,0:T(4,128)S(1)}, f32[3,8192]{1,0:T(4,128)}, u32[]{:S(2)}) copy-start(f32[3,8192]{1,0:T(4,128)} %param.17) | copy-start | bytes 294916
  0.6 17.2 %copy-start.7 = (f32[8192]{0:T(1024)S(1)}, f32[8192]{0:T(1024)}, u32[]{:S(2)}) copy-start(f32[8192]{0:T(1024)} %param.16) | copy-start | bytes 98308
  0.7 17.2 %copy-start.6 = (f32[8192]{0:T(1024)S(1)}, f32[8192]{0:T(1024)}, u32[]{:S(2)}) copy-start(f32[8192]{0:T(1024)} %param.15) | copy-start | bytes 98308
  0.7 17.2 %copy-start.5 = (f32[2,8192]{1,0:T(2,128)S(1)}, f32[2,8192]{1,0:T(2,128)}, u32[]{:S(2)}) copy-start(f32[2,8192]{1,0:T(2,128)} %param.14) | copy-start | bytes 196612
  1.6 0.7 copy-start.1
  6.3 30.6 %all-to-all-start = ((f32[128,16,128]{2,1,0:T(8,128)}), f32[128,16,128]{2,1,0:T(8,128)S(1)}, u32[]{:S(2)}, u32[]{:S(2)}) async-start(f32[128,16,128]{2,1,0:T(8,128)} %bitcast.2), calls=%async_computation | async-start | bytes 2097152 | tf_op jit(solution)/shard_map/all_to_all | solution.py:356
  18.1 18.7 %copy-start = (f32[8,8192]{1,0:T(8,128)}, f32[8,8192]{1,0:T(8,128)S(1)}, u32[]{:S(2)}) copy-start(f32[8,8192]{1,0:T(8,128)S(1)} %concatenate.13.window.own) | copy-start | bytes 786436
  22.2 9.4 %collective-permute-start.1 = (f32[8,1024]{1,0:T(8,128)S(1)}, f32[8,1024]{1,0:T(8,128)S(1)}, u32[]{:S(2)}, u32[]{:S(2)}) collective-permute-start(f32[8,1024]{1,0:T(8,128)S(1)} %get-tuple-element.36), channel_id=1, source_target_pairs={{8,0},{16,8},{24,16},{32,24},{40,32},{48,40},{56,48},{64,56},{72,6... | collective-permute-start | bytes 98312 | tf_op jit(solution)/shard_map/ppermute | solution.py:368
  23.5 8.1 %collective-permute-start = (f32[8,1024]{1,0:T(8,128)S(1)}, f32[8,1024]{1,0:T(8,128)S(1)}, u32[]{:S(2)}, u32[]{:S(2)}) collective-permute-start(f32[8,1024]{1,0:T(8,128)S(1)} %get-tuple-element.37), channel_id=1, source_target_pairs={{0,8},{8,16},{16,24},{24,32},{32,40},{40,48},{48,56},{56,64},{64,7... | collective-permute-start | bytes 98312 | tf_op jit(solution)/shard_map/ppermute | solution.py:367
  31.5 5.3 %copy-start.2 = (f32[8,1024]{1,0:T(8,128)}, f32[8,1024]{1,0:T(8,128)S(1)}, u32[]{:S(2)}) copy-start(f32[8,1024]{1,0:T(8,128)S(1)} %collective-permute-done.1.above) | copy-start | bytes 98308
  31.5 5.3 %copy-start.3 = (f32[8,1024]{1,0:T(8,128)}, f32[8,1024]{1,0:T(8,128)S(1)}, u32[]{:S(2)}) copy-start(f32[8,1024]{1,0:T(8,128)S(1)} %collective-permute-done.below) | copy-start | bytes 98308

commit v6 on v5

--- a/solution.py
+++ b/solution.py
@@ -12,7 +12,7 @@
 K = 4
 MB = 8
 CAP = 4
-UNROLL = 32
+UNROLL = 40
 GROUP = 2
 TERMS = 32
 DEAD = 127
@@ -129,7 +129,7 @@
     return order_dump(messages) + 1
 
 
-def prepare_kernel(window, far_wide, far_left, wide, left, sems):
+def prepare_kernel(start, window, far_wide, far_left, wide, left, sems):
     runs = wide.shape[0] // 4
 
     def copies(run):
@@ -142,7 +142,7 @@
     def make(run, c):
         for k in range(4):
             w = run * 4 + k
-            tile = window[:, pl.ds(pl.multiple_of(w * TB, TB), TB)]
+            tile = window[:, pl.ds(pl.multiple_of((start + w) * TB, TB), TB)]
             wide[w] = jnp.broadcast_to(-tile[5:6], (TB, TB)).T
             left[w] = left_terms(tile).T.astype(BF16)
         for copy in copies(run):
@@ -159,7 +159,7 @@
 
 
 def match_kernel(
-    a_rows, own, below, above, wide_own, left_own, wide_edge, left_edge,
+    a_rows, own, below, above, wide_first, left_first, wide_rest, left_rest, wide_edge, left_edge,
     out, window, wide, left, right, acc, order, blank, order_s, todo, sems,
 ):
     messages = a_rows.shape[0] // 16
@@ -167,9 +167,13 @@
     blocks = own.shape[1] // TB
     row = lax.broadcasted_iota(jnp.int32, (8, TB), 0)
     fetches = []
-    for edge, inner, there in ((wide_edge, wide_own, wide), (left_edge, left_own, left)):
+    early = MB + left_first.shape[0]
+    for edge, first, rest, there in (
+        (wide_edge, wide_first, wide_rest, wide), (left_edge, left_first, left_rest, left)
+    ):
         fetches.append((edge.at[0:MB], there.at[0:MB]))
-        fetches.append((inner, there.at[MB : MB + blocks]))
+        fetches.append((first, there.at[MB:early]))
+        fetches.append((rest, there.at[early : MB + blocks]))
         fetches.append((edge.at[MB : 2 * MB], there.at[MB + blocks : 2 * MB + blocks]))
     fetches.append((below, window.at[:, 0 : MB * TB]))
     fetches.append((own, window.at[:, MB * TB : (MB + blocks) * TB]))
@@ -283,10 +287,9 @@
     return [pltpu.with_memory_space_constraint(x, pltpu.HBM) for x in arrays]
 
 
-def prepare_call(window):
-    blocks = window.shape[1] // TB
+def prepare_call(window, start, blocks):
     return pl.pallas_call(
-        prepare_kernel,
+        functools.partial(prepare_kernel, start),
         out_shape=(pltpu.HBM((blocks, TB, TB), F32), pltpu.HBM((blocks, TB, TB), BF16)),
         in_specs=[VMEM],
         out_specs=(FAR, FAR),
@@ -308,7 +311,7 @@
     return pl.pallas_call(
         match_kernel,
         out_shape=jax.ShapeDtypeStruct((messages, CAP * 6, TB), F32),
-        in_specs=[VMEM] + [FAR] * 7,
+        in_specs=[VMEM] + [FAR] * 9,
         out_specs=VMEM,
         scratch_shapes=[
             pltpu.VMEM((8, blocks * TB), F32),
@@ -320,7 +323,7 @@
             pltpu.VMEM((size,), jnp.int32),
             pltpu.SMEM((24, messages), jnp.int32),
             pltpu.SMEM((size,), jnp.int32),
-            pltpu.SemaphoreType.DMA((11,)),
+            pltpu.SemaphoreType.DMA((13,)),
         ],
         compiler_params=params(28),
         name="match",
@@ -359,16 +362,18 @@
     own = jnp.concatenate(
         [b_coord, b_flux, b_var[None, :], b_prior[None, :], jnp.zeros_like(b_var)[None, :]], axis=0
     )
-    inner = prepare_call(own)
+    blocks, early = own.shape[1] // TB, 16
+    first = prepare_call(own, 0, early)
     width = MB * TB
     ends = jnp.concatenate([own[:, -width:], own[:, :width]], axis=1)
-    ends, *inner = lax.optimization_barrier((ends, *inner))
+    ends, *first = lax.optimization_barrier((ends, *first))
     up = [(i, i + 1) for i in range(zones - 1)]
     below = lax.ppermute(ends[:, :width], "zone", up)
     above = lax.ppermute(ends[:, width:], "zone", [(j, i) for i, j in up])
-    edge = prepare_call(jnp.concatenate([below, above], axis=1))
+    rest = prepare_call(own, early, blocks - early)
+    edge = prepare_call(jnp.concatenate([below, above], axis=1), 0, 2 * MB)
     slots = devices * CAP
-    result = match_call(got.reshape(devices * 16, TB), own, below, above, *inner, *edge)
+    result = match_call(got.reshape(devices * 16, TB), own, below, above, *first, *rest, *edge)
     back = lax.all_to_all(result, ("zone", "tile"), split_axis=0, concat_axis=0, tiled=True)
     matched, prob = pl.pallas_call(
         unpack_kernel,

time: 104 us -> 105 us (level)
  blocking collectives: 36.7 us -> 43.7 us
  Pallas kernels: 39.4 us -> 34.5 us
    all_to_all x1, blocking collectives: 36.7 us -> 43.7 us  [body(): lax.all_to_all(result, ('zone', 'tile'), split_axis=0, concat_axis=0, til...]
    pallas_call x1, Pallas kernels: 27.7 us -> 22 us  [match_call(): pl.pallas_call(match_kernel, out_shape=jax.ShapeDtypeStruct((messages, CA...]
    pallas_call x2 -> x3, Pallas kernels: 5.53 us -> 6.3 us  [prepare_call(): pl.pallas_call(functools.partial(prepare_kernel, start), out_shape=(pltpu...]
  transfers between devices with their start and end apart: 3 -> 3, of which waited for: 2 -> 2; matrix products, arithmetic and copies ran while one was open for 0% -> 0% of each run, Pallas kernels for 5% -> 6%
where the time goes in v6:
time: 105 us
  blocking collectives  43.7 us (42%)
  Pallas kernels  34.5 us (33%)
  starting transfers between devices  16.8 us (16%)
  waiting for transfers between devices  7.01 us (7%)
  local copies, waits for them, and re-layouts  1.14 us (1%)
    all_to_all x1, blocking collectives, body(): lax.all_to_all(result, ('zone', 'tile'), split_axis=0, concat_axis=0, til...  43.7 us
    pallas_call x1, Pallas kernels, match_call(): pl.pallas_call(match_kernel, out_shape=jax.ShapeDtypeStruct((messages, CA...  22 us
    all_to_all x1, starting transfers between devices, body(): lax.all_to_all(send.reshape(devices, 16, TB), ('zone', 'tile'), split_axi...  11.5 us
    pallas_call x3, Pallas kernels, prepare_call(): pl.pallas_call(functools.partial(prepare_kernel, start), out_shape=(pltpu...  6.3 us
    ppermute x1, starting transfers between devices, body(): below = lax.ppermute(ends[:, :width], 'zone', up)  4.04 us
    pallas_call x1, Pallas kernels, body(): pl.pallas_call(pack_kernel, out_shape=(jax.ShapeDtypeStruct((devices * 16...  3.97 us
    all_to_all x1, waiting for transfers between devices, body(): lax.all_to_all(send.reshape(devices, 16, TB), ('zone', 'tile'), split_axi...  3.74 us
    ppermute x1, waiting for transfers between devices, body(): above = lax.ppermute(ends[:, width:], 'zone', [(j, i) for i, j in up])  3.26 us
  transfers between devices with their start and end apart: 3, of which 2 were waited for; matrix products, arithmetic and copies ran while one was open for 0% of the time, Pallas kernels for 6%

profile of v6, /device:TPU:1, one launch (start us, length us, event | category | flops | bytes accessed | tf_op | source)
XLA Modules:
  0.0 104.8 jit_solution(9990262911326825353)
XLA Ops:
  0.6 0.0 copy-start.4
  0.6 0.0 copy-start.7
  0.7 0.0 copy-start.6
  0.7 0.0 copy-start.5
  0.7 0.8 add_convert_fusion
  1.4 0.1 copy.14
  1.6 0.0 copy-start.1
  1.6 0.7 copy-done.1
  2.3 4.0 %pack.1 = (f32[2048,128]{1,0:T(8,128)}, s32[256]{0:T(256)S(1)}) custom-call(s32[256]{0:T(256)S(1)} %bitcast.10, f32[2,32768]{1,0:T(2,128)} %far_coord.1, f32[256,128]{1,0:T(8,128)} %bitcast.11, f32[256,128]{1,0:T(8,128)S(1)} %pad.4.labels), custom_call_target="tpu_custom_call" | custom-call | tf_op jit(solution)/shard_map/pack/pallas_call | solution.py:339
  6.3 11.5 %all-to-all-start = ((f32[128,16,128]{2,1,0:T(8,128)}), f32[128,16,128]{2,1,0:T(8,128)S(1)}, u32[]{:S(2)}, u32[]{:S(2)}) async-start(f32[128,16,128]{2,1,0:T(8,128)} %bitcast.2), calls=%async_computation | async-start | bytes 2097152 | tf_op jit(solution)/shard_map/all_to_all | solution.py:359
  17.8 0.0 copy-done.4
  17.8 0.0 copy-done.7
  17.8 0.0 copy-done.6
  17.8 0.0 copy-done.5
  17.8 0.3 concatenate.13.window.own
  18.1 0.0 copy-start
  18.1 1.6 %prepare.3 = (f32[16,128,128]{2,1,0:T(8,128)}, bf16[16,128,128]{2,1,0:T(8,128)(2,1)}) custom-call(f32[8,8192]{1,0:T(8,128)S(1)} %concatenate.13.window.own), custom_call_target="tpu_custom_call" | custom-call | flops 100000000 | bytes 10000000 | tf_op jit(solution)/shard_map/prepare/pallas_call | solution.py:291
  19.7 1.3 %collective-permute-start.1 = (f32[8,1024]{1,0:T(8,128)S(1)}, f32[8,1024]{1,0:T(8,128)S(1)}, u32[]{:S(2)}, u32[]{:S(2)}) collective-permute-start(f32[8,1024]{1,0:T(8,128)S(1)} %get-tuple-element.40), channel_id=1, source_target_pairs={{8,0},{16,8},{24,16},{32,24},{40,32},{48,40},{56,48},{64,56},{72,6... | collective-permute-start | bytes 98312 | tf_op jit(solution)/shard_map/ppermute | solution.py:372
  21.0 4.0 %collective-permute-start = (f32[8,1024]{1,0:T(8,128)S(1)}, f32[8,1024]{1,0:T(8,128)S(1)}, u32[]{:S(2)}, u32[]{:S(2)}) collective-permute-start(f32[8,1024]{1,0:T(8,128)S(1)} %get-tuple-element.41), channel_id=1, source_target_pairs={{0,8},{8,16},{16,24},{24,32},{32,40},{40,48},{48,56},{56,64},{64,7... | collective-permute-start | bytes 98312 | tf_op jit(solution)/shard_map/ppermute | solution.py:371
  25.1 3.2 %prepare.4 = (f32[48,128,128]{2,1,0:T(8,128)}, bf16[48,128,128]{2,1,0:T(8,128)(2,1)}) custom-call(f32[8,8192]{1,0:T(8,128)S(1)} %concatenate.13.window.own), custom_call_target="tpu_custom_call" | custom-call | flops 100000000 | bytes 10000000 | tf_op jit(solution)/shard_map/prepare/pallas_call | solution.py:291
  28.3 3.3 %collective-permute-done.1.above = f32[8,1024]{1,0:T(8,128)S(1)} collective-permute-done((f32[8,1024]{1,0:T(8,128)S(1)}, f32[8,1024]{1,0:T(8,128)S(1)}, u32[]{:S(2)}, u32[]{:S(2)}) %collective-permute-start.1) | collective-permute-done | bytes 32800 | tf_op jit(solution)/shard_map/ppermute | solution.py:372
  31.5 0.0 copy-start.2
  31.5 0.0 collective-permute-done.below
  31.5 0.0 copy-start.3
  31.6 1.5 %prepare.5 = (f32[16,128,128]{2,1,0:T(8,128)}, bf16[16,128,128]{2,1,0:T(8,128)(2,1)}) custom-call(f32[8,2048]{1,0:T(8,128)S(1)} %pad_maximum_fusion.1.window), custom_call_target="tpu_custom_call" | custom-call | flops 100000000 | bytes 10000000 | tf_op jit(solution)/shard_map/prepare/pallas_call | solution.py:291
  33.1 3.7 %all-to-all-done = f32[128,16,128]{2,1,0:T(8,128)S(1)} async-done(((f32[128,16,128]{2,1,0:T(8,128)}), f32[128,16,128]{2,1,0:T(8,128)S(1)}, u32[]{:S(2)}, u32[]{:S(2)}) %all-to-all-start) | async-done | bytes 1048608 | tf_op jit(solution)/shard_map/all_to_all | solution.py:359
  36.9 0.0 copy-done
  36.9 0.0 copy-done.2
  36.9 0.0 copy-done.3
  36.9 22.0 %match.1 = f32[128,24,128]{2,1,0:T(8,128)S(1)} custom-call(f32[2048,128]{1,0:T(8,128)S(1)} %bitcast.9, f32[8,8192]{1,0:T(8,128)} %copy-done, f32[8,1024]{1,0:T(8,128)} %copy-done.3, f32[8,1024]{1,0:T(8,128)} %copy-done.2, f32[16,128,128]{2,1,0:T(8,128)} %get-tuple-element.30.wide_first, bf16[16,128,128]{2,1,0:T(8,128)(2,1)} %get-tuple-element.31.left_first, ...), custom_call_target="tpu_custom_call" | custom-call | tf_op jit(solution)/shard_map/match/pallas_call | solution.py:311
  58.8 43.7 %all_to_all.10 = f32[128,24,128]{2,1,0:T(8,128)S(1)} all-to-all(f32[128,24,128]{2,1,0:T(8,128)S(1)} %match.1), channel_id=1, replica_groups=mesh['zone'=16,'tile'=8] {'zone','tile'}, dimensions={0} | all-to-all | bytes 3145728 | tf_op jit(solution)/shard_map/all_to_all | solution.py:377
  102.5 2.2 %unpack.1 = (f32[5,32768]{1,0:T(8,128)}, f32[256,128]{1,0:T(8,128)}) custom-call(s32[256]{0:T(256)S(1)} %get-tuple-element.20.place, f32[3072,128]{1,0:T(8,128)S(1)} %bitcast.8), custom_call_target="tpu_custom_call" | custom-call | tf_op jit(solution)/shard_map/unpack/pallas_call | solution.py:378
  (6 shorter events, 0.1 us)
Async XLA Ops:
  0.6 17.2 %copy-start.4 = (f32[3,8192]{1,0:T(4,128)S(1)}, f32[3,8192]{1,0:T(4,128)}, u32[]{:S(2)}) copy-start(f32[3,8192]{1,0:T(4,128)} %param.17) | copy-start | bytes 294916
  0.6 17.2 %copy-start.7 = (f32[8192]{0:T(1024)S(1)}, f32[8192]{0:T(1024)}, u32[]{:S(2)}) copy-start(f32[8192]{0:T(1024)} %param.16) | copy-start | bytes 98308
  0.7 17.2 %copy-start.6 = (f32[8192]{0:T(1024)S(1)}, f32[8192]{0:T(1024)}, u32[]{:S(2)}) copy-start(f32[8192]{0:T(1024)} %param.15) | copy-start | bytes 98308
  0.7 17.2 %copy-start.5 = (f32[2,8192]{1,0:T(2,128)S(1)}, f32[2,8192]{1,0:T(2,128)}, u32[]{:S(2)}) copy-start(f32[2,8192]{1,0:T(2,128)} %param.14) | copy-start | bytes 196612
  1.6 0.7 copy-start.1
  6.3 30.6 %all-to-all-start = ((f32[128,16,128]{2,1,0:T(8,128)}), f32[128,16,128]{2,1,0:T(8,128)S(1)}, u32[]{:S(2)}, u32[]{:S(2)}) async-start(f32[128,16,128]{2,1,0:T(8,128)} %bitcast.2), calls=%async_computation | async-start | bytes 2097152 | tf_op jit(solution)/shard_map/all_to_all | solution.py:359
  18.1 18.7 %copy-start = (f32[8,8192]{1,0:T(8,128)}, f32[8,8192]{1,0:T(8,128)S(1)}, u32[]{:S(2)}) copy-start(f32[8,8192]{1,0:T(8,128)S(1)} %concatenate.13.window.own) | copy-start | bytes 786436
  19.7 11.8 %collective-permute-start.1 = (f32[8,1024]{1,0:T(8,128)S(1)}, f32[8,1024]{1,0:T(8,128)S(1)}, u32[]{:S(2)}, u32[]{:S(2)}) collective-permute-start(f32[8,1024]{1,0:T(8,128)S(1)} %get-tuple-element.40), channel_id=1, source_target_pairs={{8,0},{16,8},{24,16},{32,24},{40,32},{48,40},{56,48},{64,56},{72,6... | collective-permute-start | bytes 98312 | tf_op jit(solution)/shard_map/ppermute | solution.py:372
  21.0 10.5 %collective-permute-start = (f32[8,1024]{1,0:T(8,128)S(1)}, f32[8,1024]{1,0:T(8,128)S(1)}, u32[]{:S(2)}, u32[]{:S(2)}) collective-permute-start(f32[8,1024]{1,0:T(8,128)S(1)} %get-tuple-element.41), channel_id=1, source_target_pairs={{0,8},{8,16},{16,24},{24,32},{32,40},{40,48},{48,56},{56,64},{64,7... | collective-permute-start | bytes 98312 | tf_op jit(solution)/shard_map/ppermute | solution.py:371
  31.5 5.3 %copy-start.2 = (f32[8,1024]{1,0:T(8,128)}, f32[8,1024]{1,0:T(8,128)S(1)}, u32[]{:S(2)}) copy-start(f32[8,1024]{1,0:T(8,128)S(1)} %collective-permute-done.1.above) | copy-start | bytes 98308
  31.5 5.3 %copy-start.3 = (f32[8,1024]{1,0:T(8,128)}, f32[8,1024]{1,0:T(8,128)S(1)}, u32[]{:S(2)}) copy-start(f32[8,1024]{1,0:T(8,128)S(1)} %collective-permute-done.below) | copy-start | bytes 98308

commit v7 on v6

--- a/solution.py
+++ b/solution.py
@@ -12,7 +12,7 @@
 K = 4
 MB = 8
 CAP = 4
-UNROLL = 40
+UNROLL = 48
 GROUP = 2
 TERMS = 32
 DEAD = 127
@@ -362,7 +362,7 @@
     own = jnp.concatenate(
         [b_coord, b_flux, b_var[None, :], b_prior[None, :], jnp.zeros_like(b_var)[None, :]], axis=0
     )
-    blocks, early = own.shape[1] // TB, 16
+    blocks, early = own.shape[1] // TB, 4
     first = prepare_call(own, 0, early)
     width = MB * TB
     ends = jnp.concatenate([own[:, -width:], own[:, :width]], axis=1)

time: 105 us -> 104 us (level)
  blocking collectives: 43.7 us -> 41.7 us
    all_to_all x1, blocking collectives: 43.7 us -> 41.7 us  [body(): lax.all_to_all(result, ('zone', 'tile'), split_axis=0, concat_axis=0, til...]
where the time goes in v7:
time: 104 us; the launch traced here: 103 us
  blocking collectives  41.7 us (40%)
  Pallas kernels  35.2 us (34%)
  starting transfers between devices  16.8 us (16%)
  waiting for transfers between devices  6.98 us (7%)
  local copies, waits for them, and re-layouts  1.14 us (1%)
    all_to_all x1, blocking collectives, body(): lax.all_to_all(result, ('zone', 'tile'), split_axis=0, concat_axis=0, til...  41.7 us
    pallas_call x1, Pallas kernels, match_call(): pl.pallas_call(match_kernel, out_shape=jax.ShapeDtypeStruct((messages, CA...  22.6 us
    all_to_all x1, starting transfers between devices, body(): lax.all_to_all(send.reshape(devices, 16, TB), ('zone', 'tile'), split_axi...  11.5 us
    pallas_call x3, Pallas kernels, prepare_call(): pl.pallas_call(functools.partial(prepare_kernel, start), out_shape=(pltpu...  6.33 us
    ppermute x1, starting transfers between devices, body(): below = lax.ppermute(ends[:, :width], 'zone', up)  4.04 us
    pallas_call x1, Pallas kernels, body(): pl.pallas_call(pack_kernel, out_shape=(jax.ShapeDtypeStruct((devices * 16...  3.97 us
    all_to_all x1, waiting for transfers between devices, body(): lax.all_to_all(send.reshape(devices, 16, TB), ('zone', 'tile'), split_axi...  3.75 us
    ppermute x1, waiting for transfers between devices, body(): above = lax.ppermute(ends[:, width:], 'zone', [(j, i) for i, j in up])  3.23 us
  transfers between devices with their start and end apart: 3, of which 2 were waited for; matrix products, arithmetic and copies ran while one was open for 0% of the time, Pallas kernels for 6%

profile of v7, /device:TPU:1, one launch (start us, length us, event | category | flops | bytes accessed | tf_op | source)
XLA Modules:
  0.0 103.4 jit_solution(6566237743266336769)
XLA Ops:
  0.6 0.0 copy-start.4
  0.6 0.0 copy-start.7
  0.7 0.0 copy-start.6
  0.7 0.0 copy-start.5
  0.7 0.8 add_convert_fusion
  1.4 0.1 copy.14
  1.6 0.0 copy-start.1
  1.6 0.7 copy-done.1
  2.3 4.0 %pack.1 = (f32[2048,128]{1,0:T(8,128)}, s32[256]{0:T(256)S(1)}) custom-call(s32[256]{0:T(256)S(1)} %bitcast.10, f32[2,32768]{1,0:T(2,128)} %far_coord.1, f32[256,128]{1,0:T(8,128)} %bitcast.11, f32[256,128]{1,0:T(8,128)S(1)} %pad.4.labels), custom_call_target="tpu_custom_call" | custom-call | tf_op jit(solution)/shard_map/pack/pallas_call | solution.py:339
  6.3 11.5 %all-to-all-start = ((f32[128,16,128]{2,1,0:T(8,128)}), f32[128,16,128]{2,1,0:T(8,128)S(1)}, u32[]{:S(2)}, u32[]{:S(2)}) async-start(f32[128,16,128]{2,1,0:T(8,128)} %bitcast.2), calls=%async_computation | async-start | bytes 2097152 | tf_op jit(solution)/shard_map/all_to_all | solution.py:359
  17.8 0.0 copy-done.4
  17.8 0.0 copy-done.7
  17.8 0.0 copy-done.6
  17.8 0.0 copy-done.5
  17.8 0.3 concatenate.13.window.own
  18.1 0.0 copy-start
  18.1 0.9 prepare.3
  19.1 1.3 %collective-permute-start.1 = (f32[8,1024]{1,0:T(8,128)S(1)}, f32[8,1024]{1,0:T(8,128)S(1)}, u32[]{:S(2)}, u32[]{:S(2)}) collective-permute-start(f32[8,1024]{1,0:T(8,128)S(1)} %get-tuple-element.40), channel_id=1, source_target_pairs={{8,0},{16,8},{24,16},{32,24},{40,32},{48,40},{56,48},{64,56},{72,6... | collective-permute-start | bytes 98312 | tf_op jit(solution)/shard_map/ppermute | solution.py:372
  20.4 4.0 %collective-permute-start = (f32[8,1024]{1,0:T(8,128)S(1)}, f32[8,1024]{1,0:T(8,128)S(1)}, u32[]{:S(2)}, u32[]{:S(2)}) collective-permute-start(f32[8,1024]{1,0:T(8,128)S(1)} %get-tuple-element.41), channel_id=1, source_target_pairs={{0,8},{8,16},{16,24},{24,32},{32,40},{40,48},{48,56},{56,64},{64,7... | collective-permute-start | bytes 98312 | tf_op jit(solution)/shard_map/ppermute | solution.py:371
  24.5 3.8 %prepare.4 = (f32[60,128,128]{2,1,0:T(8,128)}, bf16[60,128,128]{2,1,0:T(8,128)(2,1)}) custom-call(f32[8,8192]{1,0:T(8,128)S(1)} %concatenate.13.window.own), custom_call_target="tpu_custom_call" | custom-call | flops 100000000 | bytes 10000000 | tf_op jit(solution)/shard_map/prepare/pallas_call | solution.py:291
  28.3 3.2 %collective-permute-done.1.above = f32[8,1024]{1,0:T(8,128)S(1)} collective-permute-done((f32[8,1024]{1,0:T(8,128)S(1)}, f32[8,1024]{1,0:T(8,128)S(1)}, u32[]{:S(2)}, u32[]{:S(2)}) %collective-permute-start.1) | collective-permute-done | bytes 32800 | tf_op jit(solution)/shard_map/ppermute | solution.py:372
  31.5 0.0 copy-start.2
  31.5 0.0 collective-permute-done.below
  31.5 0.0 copy-start.3
  31.5 1.6 %prepare.5 = (f32[16,128,128]{2,1,0:T(8,128)}, bf16[16,128,128]{2,1,0:T(8,128)(2,1)}) custom-call(f32[8,2048]{1,0:T(8,128)S(1)} %pad_maximum_fusion.1.window), custom_call_target="tpu_custom_call" | custom-call | flops 100000000 | bytes 10000000 | tf_op jit(solution)/shard_map/prepare/pallas_call | solution.py:291
  33.1 3.7 %all-to-all-done = f32[128,16,128]{2,1,0:T(8,128)S(1)} async-done(((f32[128,16,128]{2,1,0:T(8,128)}), f32[128,16,128]{2,1,0:T(8,128)S(1)}, u32[]{:S(2)}, u32[]{:S(2)}) %all-to-all-start) | async-done | bytes 1048608 | tf_op jit(solution)/shard_map/all_to_all | solution.py:359
  36.9 0.0 copy-done
  36.9 0.0 copy-done.2
  36.9 0.0 copy-done.3
  36.9 22.6 %match.1 = f32[128,24,128]{2,1,0:T(8,128)S(1)} custom-call(f32[2048,128]{1,0:T(8,128)S(1)} %bitcast.9, f32[8,8192]{1,0:T(8,128)} %copy-done, f32[8,1024]{1,0:T(8,128)} %copy-done.3, f32[8,1024]{1,0:T(8,128)} %copy-done.2, f32[4,128,128]{2,1,0:T(8,128)} %get-tuple-element.30.wide_first, bf16[4,128,128]{2,1,0:T(8,128)(2,1)} %get-tuple-element.31.left_first, ...), custom_call_target="tpu_custom_call" | custom-call | tf_op jit(solution)/shard_map/match/pallas_call | solution.py:311
  59.5 41.7 %all_to_all.10 = f32[128,24,128]{2,1,0:T(8,128)S(1)} all-to-all(f32[128,24,128]{2,1,0:T(8,128)S(1)} %match.1), channel_id=1, replica_groups=mesh['zone'=16,'tile'=8] {'zone','tile'}, dimensions={0} | all-to-all | bytes 3145728 | tf_op jit(solution)/shard_map/all_to_all | solution.py:377
  101.2 2.2 %unpack.1 = (f32[5,32768]{1,0:T(8,128)}, f32[256,128]{1,0:T(8,128)}) custom-call(s32[256]{0:T(256)S(1)} %get-tuple-element.20.place, f32[3072,128]{1,0:T(8,128)S(1)} %bitcast.8), custom_call_target="tpu_custom_call" | custom-call | tf_op jit(solution)/shard_map/unpack/pallas_call | solution.py:378
  (6 shorter events, 0.1 us)
Async XLA Ops:
  0.6 17.2 %copy-start.4 = (f32[3,8192]{1,0:T(4,128)S(1)}, f32[3,8192]{1,0:T(4,128)}, u32[]{:S(2)}) copy-start(f32[3,8192]{1,0:T(4,128)} %param.17) | copy-start | bytes 294916
  0.6 17.2 %copy-start.7 = (f32[8192]{0:T(1024)S(1)}, f32[8192]{0:T(1024)}, u32[]{:S(2)}) copy-start(f32[8192]{0:T(1024)} %param.16) | copy-start | bytes 98308
  0.7 17.2 %copy-start.6 = (f32[8192]{0:T(1024)S(1)}, f32[8192]{0:T(1024)}, u32[]{:S(2)}) copy-start(f32[8192]{0:T(1024)} %param.15) | copy-start | bytes 98308
  0.7 17.2 %copy-start.5 = (f32[2,8192]{1,0:T(2,128)S(1)}, f32[2,8192]{1,0:T(2,128)}, u32[]{:S(2)}) copy-start(f32[2,8192]{1,0:T(2,128)} %param.14) | copy-start | bytes 196612
  1.6 0.7 copy-start.1
  6.3 30.6 %all-to-all-start = ((f32[128,16,128]{2,1,0:T(8,128)}), f32[128,16,128]{2,1,0:T(8,128)S(1)}, u32[]{:S(2)}, u32[]{:S(2)}) async-start(f32[128,16,128]{2,1,0:T(8,128)} %bitcast.2), calls=%async_computation | async-start | bytes 2097152 | tf_op jit(solution)/shard_map/all_to_all | solution.py:359
  18.1 18.7 %copy-start = (f32[8,8192]{1,0:T(8,128)}, f32[8,8192]{1,0:T(8,128)S(1)}, u32[]{:S(2)}) copy-start(f32[8,8192]{1,0:T(8,128)S(1)} %concatenate.13.window.own) | copy-start | bytes 786436
  19.1 12.4 %collective-permute-start.1 = (f32[8,1024]{1,0:T(8,128)S(1)}, f32[8,1024]{1,0:T(8,128)S(1)}, u32[]{:S(2)}, u32[]{:S(2)}) collective-permute-start(f32[8,1024]{1,0:T(8,128)S(1)} %get-tuple-element.40), channel_id=1, source_target_pairs={{8,0},{16,8},{24,16},{32,24},{40,32},{48,40},{56,48},{64,56},{72,6... | collective-permute-start | bytes 98312 | tf_op jit(solution)/shard_map/ppermute | solution.py:372
  20.4 11.1 %collective-permute-start = (f32[8,1024]{1,0:T(8,128)S(1)}, f32[8,1024]{1,0:T(8,128)S(1)}, u32[]{:S(2)}, u32[]{:S(2)}) collective-permute-start(f32[8,1024]{1,0:T(8,128)S(1)} %get-tuple-element.41), channel_id=1, source_target_pairs={{0,8},{8,16},{16,24},{24,32},{32,40},{40,48},{48,56},{56,64},{64,7... | collective-permute-start | bytes 98312 | tf_op jit(solution)/shard_map/ppermute | solution.py:371
  31.5 5.3 %copy-start.2 = (f32[8,1024]{1,0:T(8,128)}, f32[8,1024]{1,0:T(8,128)S(1)}, u32[]{:S(2)}) copy-start(f32[8,1024]{1,0:T(8,128)S(1)} %collective-permute-done.1.above) | copy-start | bytes 98308
  31.5 5.3 %copy-start.3 = (f32[8,1024]{1,0:T(8,128)}, f32[8,1024]{1,0:T(8,128)S(1)}, u32[]{:S(2)}) copy-start(f32[8,1024]{1,0:T(8,128)S(1)} %collective-permute-done.below) | copy-start | bytes 98308

commit v8 on v6

--- a/solution.py
+++ b/solution.py
@@ -259,7 +259,7 @@
         out[m] = jnp.concatenate(parts, axis=0)
         return carry
 
-    lax.fori_loop(0, messages, finish, 0, unroll=2)
+    lax.fori_loop(0, messages, finish, 0, unroll=8)
 
 
 def unpack_kernel(place, back, matched, prob):
@@ -271,7 +271,7 @@
         prob[pl.ds(b, 1), :] = back[pl.ds(base + 5, 1), :]
         return c
 
-    lax.fori_loop(0, place.shape[0], one, 0, unroll=8)
+    lax.fori_loop(0, place.shape[0], one, 0, unroll=16)
 
 
 VMEM = pl.BlockSpec(memory_space=pltpu.VMEM)

time: 105 us -> 102 us (0.971)
  blocking collectives: 43.7 us -> 41.8 us
    all_to_all x1, blocking collectives: 43.7 us -> 41.8 us  [body(): lax.all_to_all(result, ('zone', 'tile'), split_axis=0, concat_axis=0, til...]
where the time goes in v8:
time: 102 us
  blocking collectives  41.8 us (41%)
  Pallas kernels  33.8 us (33%)
  starting transfers between devices  16.8 us (16%)
  waiting for transfers between devices  7.01 us (7%)
  local copies, waits for them, and re-layouts  1.14 us (1%)
    all_to_all x1, blocking collectives, body(): lax.all_to_all(result, ('zone', 'tile'), split_axis=0, concat_axis=0, til...  41.8 us
    pallas_call x1, Pallas kernels, match_call(): pl.pallas_call(match_kernel, out_shape=jax.ShapeDtypeStruct((messages, CA...  21.4 us
    all_to_all x1, starting transfers between devices, body(): lax.all_to_all(send.reshape(devices, 16, TB), ('zone', 'tile'), split_axi...  11.5 us
    pallas_call x3, Pallas kernels, prepare_call(): pl.pallas_call(functools.partial(prepare_kernel, start), out_shape=(pltpu...  6.3 us
    ppermute x1, starting transfers between devices, body(): below = lax.ppermute(ends[:, :width], 'zone', up)  4.04 us
    pallas_call x1, Pallas kernels, body(): pl.pallas_call(pack_kernel, out_shape=(jax.ShapeDtypeStruct((devices * 16...  3.97 us
    all_to_all x1, waiting for transfers between devices, body(): lax.all_to_all(send.reshape(devices, 16, TB), ('zone', 'tile'), split_axi...  3.74 us
    ppermute x1, waiting for transfers between devices, body(): above = lax.ppermute(ends[:, width:], 'zone', [(j, i) for i, j in up])  3.26 us
  transfers between devices with their start and end apart: 3, of which 2 were waited for; matrix products, arithmetic and copies ran while one was open for 0% of the time, Pallas kernels for 6%

profile of v8, /device:TPU:1, one launch (start us, length us, event | category | flops | bytes accessed | tf_op | source)
XLA Modules:
  0.0 102.2 jit_solution(13218446265017838719)
XLA Ops:
  0.6 0.0 copy-start.4
  0.6 0.0 copy-start.7
  0.7 0.0 copy-start.6
  0.7 0.0 copy-start.5
  0.7 0.8 add_convert_fusion
  1.4 0.1 copy.14
  1.6 0.0 copy-start.1
  1.6 0.7 copy-done.1
  2.3 4.0 %pack.1 = (f32[2048,128]{1,0:T(8,128)}, s32[256]{0:T(256)S(1)}) custom-call(s32[256]{0:T(256)S(1)} %bitcast.10, f32[2,32768]{1,0:T(2,128)} %far_coord.1, f32[256,128]{1,0:T(8,128)} %bitcast.11, f32[256,128]{1,0:T(8,128)S(1)} %pad.4.labels), custom_call_target="tpu_custom_call" | custom-call | tf_op jit(solution)/shard_map/pack/pallas_call | solution.py:339
  6.3 11.5 %all-to-all-start = ((f32[128,16,128]{2,1,0:T(8,128)}), f32[128,16,128]{2,1,0:T(8,128)S(1)}, u32[]{:S(2)}, u32[]{:S(2)}) async-start(f32[128,16,128]{2,1,0:T(8,128)} %bitcast.2), calls=%async_computation | async-start | bytes 2097152 | tf_op jit(solution)/shard_map/all_to_all | solution.py:359
  17.8 0.0 copy-done.4
  17.8 0.0 copy-done.7
  17.8 0.0 copy-done.6
  17.8 0.0 copy-done.5
  17.8 0.3 concatenate.13.window.own
  18.1 0.0 copy-start
  18.1 1.6 %prepare.3 = (f32[16,128,128]{2,1,0:T(8,128)}, bf16[16,128,128]{2,1,0:T(8,128)(2,1)}) custom-call(f32[8,8192]{1,0:T(8,128)S(1)} %concatenate.13.window.own), custom_call_target="tpu_custom_call" | custom-call | flops 100000000 | bytes 10000000 | tf_op jit(solution)/shard_map/prepare/pallas_call | solution.py:291
  19.7 1.3 %collective-permute-start.1 = (f32[8,1024]{1,0:T(8,128)S(1)}, f32[8,1024]{1,0:T(8,128)S(1)}, u32[]{:S(2)}, u32[]{:S(2)}) collective-permute-start(f32[8,1024]{1,0:T(8,128)S(1)} %get-tuple-element.40), channel_id=1, source_target_pairs={{8,0},{16,8},{24,16},{32,24},{40,32},{48,40},{56,48},{64,56},{72,6... | collective-permute-start | bytes 98312 | tf_op jit(solution)/shard_map/ppermute | solution.py:372
  21.0 4.0 %collective-permute-start = (f32[8,1024]{1,0:T(8,128)S(1)}, f32[8,1024]{1,0:T(8,128)S(1)}, u32[]{:S(2)}, u32[]{:S(2)}) collective-permute-start(f32[8,1024]{1,0:T(8,128)S(1)} %get-tuple-element.41), channel_id=1, source_target_pairs={{0,8},{8,16},{16,24},{24,32},{32,40},{40,48},{48,56},{56,64},{64,7... | collective-permute-start | bytes 98312 | tf_op jit(solution)/shard_map/ppermute | solution.py:371
  25.1 3.2 %prepare.4 = (f32[48,128,128]{2,1,0:T(8,128)}, bf16[48,128,128]{2,1,0:T(8,128)(2,1)}) custom-call(f32[8,8192]{1,0:T(8,128)S(1)} %concatenate.13.window.own), custom_call_target="tpu_custom_call" | custom-call | flops 100000000 | bytes 10000000 | tf_op jit(solution)/shard_map/prepare/pallas_call | solution.py:291
  28.3 3.3 %collective-permute-done.1.above = f32[8,1024]{1,0:T(8,128)S(1)} collective-permute-done((f32[8,1024]{1,0:T(8,128)S(1)}, f32[8,1024]{1,0:T(8,128)S(1)}, u32[]{:S(2)}, u32[]{:S(2)}) %collective-permute-start.1) | collective-permute-done | bytes 32800 | tf_op jit(solution)/shard_map/ppermute | solution.py:372
  31.5 0.0 copy-start.2
  31.5 0.0 collective-permute-done.below
  31.5 0.0 copy-start.3
  31.6 1.5 %prepare.5 = (f32[16,128,128]{2,1,0:T(8,128)}, bf16[16,128,128]{2,1,0:T(8,128)(2,1)}) custom-call(f32[8,2048]{1,0:T(8,128)S(1)} %pad_maximum_fusion.1.window), custom_call_target="tpu_custom_call" | custom-call | flops 100000000 | bytes 10000000 | tf_op jit(solution)/shard_map/prepare/pallas_call | solution.py:291
  33.1 3.7 %all-to-all-done = f32[128,16,128]{2,1,0:T(8,128)S(1)} async-done(((f32[128,16,128]{2,1,0:T(8,128)}), f32[128,16,128]{2,1,0:T(8,128)S(1)}, u32[]{:S(2)}, u32[]{:S(2)}) %all-to-all-start) | async-done | bytes 1048608 | tf_op jit(solution)/shard_map/all_to_all | solution.py:359
  36.9 0.0 copy-done
  36.9 0.0 copy-done.2
  36.9 0.0 copy-done.3
  36.9 21.4 %match.1 = f32[128,24,128]{2,1,0:T(8,128)S(1)} custom-call(f32[2048,128]{1,0:T(8,128)S(1)} %bitcast.9, f32[8,8192]{1,0:T(8,128)} %copy-done, f32[8,1024]{1,0:T(8,128)} %copy-done.3, f32[8,1024]{1,0:T(8,128)} %copy-done.2, f32[16,128,128]{2,1,0:T(8,128)} %get-tuple-element.30.wide_first, bf16[16,128,128]{2,1,0:T(8,128)(2,1)} %get-tuple-element.31.left_first, ...), custom_call_target="tpu_custom_call" | custom-call | tf_op jit(solution)/shard_map/match/pallas_call | solution.py:311
  58.3 41.8 %all_to_all.10 = f32[128,24,128]{2,1,0:T(8,128)S(1)} all-to-all(f32[128,24,128]{2,1,0:T(8,128)S(1)} %match.1), channel_id=1, replica_groups=mesh['zone'=16,'tile'=8] {'zone','tile'}, dimensions={0} | all-to-all | bytes 3145728 | tf_op jit(solution)/shard_map/all_to_all | solution.py:377
  100.1 2.2 %unpack.1 = (f32[5,32768]{1,0:T(8,128)}, f32[256,128]{1,0:T(8,128)}) custom-call(s32[256]{0:T(256)S(1)} %get-tuple-element.20.place, f32[3072,128]{1,0:T(8,128)S(1)} %bitcast.8), custom_call_target="tpu_custom_call" | custom-call | tf_op jit(solution)/shard_map/unpack/pallas_call | solution.py:378
  (6 shorter events, 0.1 us)
Async XLA Ops:
  0.6 17.2 %copy-start.4 = (f32[3,8192]{1,0:T(4,128)S(1)}, f32[3,8192]{1,0:T(4,128)}, u32[]{:S(2)}) copy-start(f32[3,8192]{1,0:T(4,128)} %param.17) | copy-start | bytes 294916
  0.6 17.2 %copy-start.7 = (f32[8192]{0:T(1024)S(1)}, f32[8192]{0:T(1024)}, u32[]{:S(2)}) copy-start(f32[8192]{0:T(1024)} %param.16) | copy-start | bytes 98308
  0.7 17.2 %copy-start.6 = (f32[8192]{0:T(1024)S(1)}, f32[8192]{0:T(1024)}, u32[]{:S(2)}) copy-start(f32[8192]{0:T(1024)} %param.15) | copy-start | bytes 98308
  0.7 17.2 %copy-start.5 = (f32[2,8192]{1,0:T(2,128)S(1)}, f32[2,8192]{1,0:T(2,128)}, u32[]{:S(2)}) copy-start(f32[2,8192]{1,0:T(2,128)} %param.14) | copy-start | bytes 196612
  1.6 0.7 copy-start.1
  6.3 30.6 %all-to-all-start = ((f32[128,16,128]{2,1,0:T(8,128)}), f32[128,16,128]{2,1,0:T(8,128)S(1)}, u32[]{:S(2)}, u32[]{:S(2)}) async-start(f32[128,16,128]{2,1,0:T(8,128)} %bitcast.2), calls=%async_computation | async-start | bytes 2097152 | tf_op jit(solution)/shard_map/all_to_all | solution.py:359
  18.1 18.7 %copy-start = (f32[8,8192]{1,0:T(8,128)}, f32[8,8192]{1,0:T(8,128)S(1)}, u32[]{:S(2)}) copy-start(f32[8,8192]{1,0:T(8,128)S(1)} %concatenate.13.window.own) | copy-start | bytes 786436
  19.7 11.8 %collective-permute-start.1 = (f32[8,1024]{1,0:T(8,128)S(1)}, f32[8,1024]{1,0:T(8,128)S(1)}, u32[]{:S(2)}, u32[]{:S(2)}) collective-permute-start(f32[8,1024]{1,0:T(8,128)S(1)} %get-tuple-element.40), channel_id=1, source_target_pairs={{8,0},{16,8},{24,16},{32,24},{40,32},{48,40},{56,48},{64,56},{72,6... | collective-permute-start | bytes 98312 | tf_op jit(solution)/shard_map/ppermute | solution.py:372
  21.0 10.5 %collective-permute-start = (f32[8,1024]{1,0:T(8,128)S(1)}, f32[8,1024]{1,0:T(8,128)S(1)}, u32[]{:S(2)}, u32[]{:S(2)}) collective-permute-start(f32[8,1024]{1,0:T(8,128)S(1)} %get-tuple-element.41), channel_id=1, source_target_pairs={{0,8},{8,16},{16,24},{24,32},{32,40},{40,48},{48,56},{56,64},{64,7... | collective-permute-start | bytes 98312 | tf_op jit(solution)/shard_map/ppermute | solution.py:371
  31.5 5.3 %copy-start.2 = (f32[8,1024]{1,0:T(8,128)}, f32[8,1024]{1,0:T(8,128)S(1)}, u32[]{:S(2)}) copy-start(f32[8,1024]{1,0:T(8,128)S(1)} %collective-permute-done.1.above) | copy-start | bytes 98308
  31.5 5.3 %copy-start.3 = (f32[8,1024]{1,0:T(8,128)}, f32[8,1024]{1,0:T(8,128)S(1)}, u32[]{:S(2)}) copy-start(f32[8,1024]{1,0:T(8,128)S(1)} %collective-permute-done.below) | copy-start | bytes 98308
